TPU v7x, 32 devices: a whole 2x2x4 slice. The times are simulated.
32 devices in a mesh: ctx: 8 (over y, x, core), head: 4 (over z).
Axes of the slice: x: 2, y: 2, z: 4, core: 2. Of those that a mesh axis runs over, the one named last changes fastest.
Arguments:
- query_rows: bfloat16 [4096, 16, 128], P('ctx', 'head'), may hold values from -45 to 45
- key_rows: bfloat16 [4096, 16, 128], P('ctx', 'head'), may hold values from -7 to 7
- value_rows: bfloat16 [4096, 16, 128], P('ctx', 'head'), may hold values from -6 to 6
- out_grad: bfloat16 [4096, 16, 128], P('ctx', 'head'), may hold values from -6 to 6
- global_pos: int32 [256], replicated, may hold values from 0 to 4095, as said below
Outputs:
- attn_out: bfloat16 [4096, 16, 128], P('ctx', 'head')
- query_grad: float32 [4096, 16, 128], P('ctx', 'head')
- key_grad: float32 [4096, 16, 128], P('ctx', 'head')
- value_grad: float32 [4096, 16, 128], P('ctx', 'head')
Inputs may be any that keep to these rules, and one draw needn't show every extreme that they name: `global_pos`: distinct positions; the aligned block of 512 positions that holds the most of them holds exactly 64, and the other blocks hold counts that differ by at most one.
All inputs are finite; a program needn't handle non-finite values.
Results may differ from a plain program's by a relative error of at most 0.03.
Values may be sent and summed in bfloat16 or wider, within the bound.
No kernel may reach another device: no remote copies, remote signals or barrier semaphores. Data moves between devices by JAX's collectives and lax.ppermute only.
A program may use at most 128 MiB of HBM per device.

v0:
```python
import functools
import math

import jax
import jax.numpy as jnp
from jax import lax
from jax.experimental import pallas as pl
from jax.experimental.pallas import tpu as pltpu
from jax.sharding import PartitionSpec as P

HALF = 512
TILE = 256
NEG = -1e30
LOG2E = 1.0 / math.log(2.0)
VMEM_BYTES = 63 * 1024 * 1024
BF = jnp.bfloat16
F32 = jnp.float32


def nt(a, b):
    return lax.dot_general(a, b, (((1,), (1,)), ((), ())), preferred_element_type=F32)


def nn(a, b):
    return lax.dot_general(a, b, (((1,), (0,)), ((), ())), preferred_element_type=F32)


def wide(column, width):
    return jnp.concatenate([column] * (width // column.shape[1]), axis=1)


def iota(shape, dim):
    return lax.broadcasted_iota(jnp.int32, shape, dim)


def params():
    return pltpu.CompilerParams(vmem_limit_bytes=VMEM_BYTES)


def as_column(row):
    return jnp.broadcast_to(row, (128, row.shape[1])).T[:, :1]


def pack_keys_kernel(heads, k, v, kv, wide_rows):
    toks = k.shape[0] // heads
    for number, source in enumerate((k, v)):
        wide_rows[number] = source[...].astype(F32)
        for head in range(heads):
            kv[number, head] = wide_rows[number, pl.ds(head, toks, stride=heads), :].astype(BF)


def pack_queries_kernel(heads, slots, q, g, kv, pos_row, qd, slot_rows, wide_rows, acc):
    step = pl.program_id(0)
    toks = q.shape[0] // heads
    row = pos_row[...]
    count = row.shape[1]
    base = lax.axis_index("ctx") * (toks * pl.num_programs(0))
    column = as_column(row)
    tok = iota((count, toks), 1) + (base + step * toks)
    hit = jnp.sum((column == tok).astype(F32), axis=0, keepdims=True)
    rank = jnp.sum(((column >= base) & (column < tok)).astype(F32), axis=0, keepdims=True)
    slot = iota((slots, toks), 0).astype(F32)
    pick = jnp.where((hit > 0) & (rank == slot), 1.0, 0.0).astype(BF)
    tok = iota((toks, count), 0) + (base + step * toks)
    hit_column = jnp.sum((row == tok).astype(F32), axis=1, keepdims=True)
    tables = [[], [kv[0, h] for h in range(heads)], [kv[1, h] for h in range(heads)], []]
    for number, source in ((0, q), (3, g)):
        wide_rows[number // 3] = source[...].astype(F32)
        for head in range(heads):
            rows = wide_rows[number // 3, pl.ds(head, toks, stride=heads), :]
            tables[number].append(rows.astype(BF))
            if number == 0:
                qd[0, head] = rows.astype(BF)
            else:
                qd[1, head] = jnp.where(hit_column > 0, 0.0, rows).astype(BF)
    for number in range(4):
        found = nn(pick, jnp.concatenate(tables[number], axis=1))
        for head in range(heads):
            part = found[:, head * 128 : (head + 1) * 128]
            acc[number, head] = jnp.where(step == 0, part, acc[number, head] + part)

    @pl.when(step == pl.num_programs(0) - 1)
    def _():
        slot_rows[...] = acc[...].astype(BF)


def mask_kernel(orders, slots, seq_rows, pos_row, bias, bias_row, compact, expand, place):
    toks = place.shape[0]
    me = lax.axis_index("ctx")
    base = me * toks
    row = pos_row[...]
    count = row.shape[1]
    column = as_column(row)
    for start in range(0, bias.shape[0], TILE):
        key = iota((TILE, count), 0) + (base - HALF + start)
        hits = jnp.sum((row == key).astype(F32), axis=1, keepdims=True)
        key = key[:, :1]
        out = (hits > 0) | (key < 0) | (key >= seq_rows)
        bias[start : start + TILE, :] = jnp.broadcast_to(jnp.where(out, NEG, 0.0), (TILE, 128))
        key = iota((count, TILE), 1) + (base - HALF + start)
        hits = jnp.sum((column == key).astype(F32), axis=0, keepdims=True)
        key = key[0:1, :]
        out = (hits > 0) | (key < 0) | (key >= seq_rows)
        shape = (8, TILE)
        bias_row[:, start : start + TILE] = jnp.broadcast_to(jnp.where(out, NEG, 0.0), shape)
    tok = iota((toks, count), 0) + base
    hit = jnp.sum((row == tok).astype(F32), axis=1, keepdims=True)
    rank = jnp.sum(((row >= base) & (row < tok)).astype(F32), axis=1, keepdims=True)
    slot = iota((toks, slots), 1).astype(F32)
    place[...] = jnp.where((hit > 0) & (rank == slot), 1.0, 0.0).astype(BF)
    for part, (first, second) in enumerate(zip(*orders)):
        low = (me ^ jnp.where(me % 2 == 0, first, second)) * toks
        inside = jnp.sum((column < low).astype(jnp.int32), axis=0, keepdims=True)
        held = jnp.sum((column < low + toks).astype(jnp.int32), axis=0, keepdims=True) - inside
        slot = iota((slots, count), 0)
        target = iota((slots, count), 1)
        hot = (target == inside + slot) & (slot < held)
        expand[part * slots : (part + 1) * slots, :] = jnp.where(hot, 1.0, 0.0).astype(BF)
    compact[...] = expand[...].astype(F32).T.astype(BF)


def stats_kernel(scale2, compact, *refs):
    parts, (kv, rows, stats) = refs[:-3], refs[-3:]
    pieces = []
    for part in parts:
        for i in range(part.shape[0]):
            pieces.append(jnp.concatenate([part[i, number, 0] for number in range(4)], axis=1))
    packed = nn(compact[...], jnp.concatenate(pieces, axis=0)).astype(BF)
    width = kv.shape[3]
    table = [packed[:, number * width : (number + 1) * width] for number in range(4)]
    for number in range(4):
        rows[number, 0] = table[number]
    queries, _, _, grads = table
    scores = nt(kv[0, 0], queries) * scale2
    top = jnp.max(scores, axis=0, keepdims=True)
    weights = jnp.exp2(scores - top)
    stats[0, 0, 0:1, :] = top
    stats[0, 0, 1:2, :] = jnp.sum(weights, axis=0, keepdims=True)
    stats[0, 0, 2:3, :] = jnp.sum(weights * nt(kv[1, 0], grads), axis=0, keepdims=True)


def band(scores, low):
    rows, columns = iota(scores.shape, 0), iota(scores.shape, 1)
    return jnp.where(rows <= columns if low else rows >= columns, scores, NEG)


def join(blocks, number, buf):
    toks = blocks[0].shape[2]
    for place, block in enumerate(blocks):
        buf[place * toks : (place + 1) * toks, :] = block[number, 0]


def forward_kernel(
    scale2, qd, left, own, right, rows, bias, out, log_dot, keys, values, score_buf, prob_buf
):
    toks = own.shape[2]
    reach = 2 * HALF + TILE
    join((left, own, right), 0, keys)
    join((left, own, right), 1, values)
    global_keys, global_values = rows[1, 0], rows[2, 0]
    count = global_keys.shape[0]
    for q_tile in range(toks // TILE):
        lanes = slice(q_tile * TILE, (q_tile + 1) * TILE)
        query = qd[0, 0, lanes, :]
        best = None
        for piece in range(reach // TILE + 1):
            spot = slice(piece * TILE, (piece + 1) * TILE)
            start = (q_tile + piece) * TILE
            if piece < reach // TILE:
                scores = nt(query, keys[start : start + TILE, :]) * scale2
                scores = scores + bias[0:1, start : start + TILE]
                if piece == 0:
                    scores = band(scores, True)
                elif piece == reach // TILE - 1:
                    scores = band(scores, False)
            else:
                scores = nt(query, global_keys) * scale2
                spot = slice(piece * TILE, piece * TILE + count)
            score_buf[:, spot] = scores
            for lane in range(0, scores.shape[1], 128):
                part = scores[:, lane : lane + 128]
                best = part if best is None else jnp.maximum(best, part)
        top = jnp.max(best, axis=1, keepdims=True)
        total = None
        for lane in range(0, reach + count, 128):
            weights = jnp.exp2(score_buf[:, lane : lane + 128] - top)
            prob_buf[:, lane : lane + 128] = weights.astype(BF)
            total = weights if total is None else total + weights
        total = jnp.sum(total, axis=1, keepdims=True)
        acc = nn(prob_buf[:, 0:reach], values[q_tile * TILE : q_tile * TILE + reach, :])
        acc = acc + nn(prob_buf[:, reach : reach + count], global_values)
        acc = acc / total
        out[0, lanes, :] = acc.astype(BF)
        dot = jnp.sum(qd[1, 0, lanes, :].astype(F32) * acc, axis=1, keepdims=True)
        lane = iota((TILE, 128), 1)
        pair = jnp.where(lane == 0, top + jnp.log2(total), jnp.where(lane == 1, dot, 0.0))
        log_dot[0, :, lanes] = pair.T[0:2, :]


def global_kernel(scale, scale2, slots, qd, own, rows, log_dot, stats, expand, dkv, sums):
    toks = own.shape[2]
    g_query, g_key, g_value, g_grad = (rows[i, 0] for i in range(4))
    tops = stats[:, 0, 0:1, :]
    top = jnp.max(tops, axis=0)
    factor = jnp.exp2(tops - top[None])
    total = jnp.sum(stats[:, 0, 1:2, :] * factor, axis=0)
    g_dot = jnp.sum(stats[:, 0, 2:3, :] * factor, axis=0) / total
    g_log = top + jnp.log2(total)
    weights = jnp.exp2(nt(own[0, 0], g_query) * scale2 - g_log)
    narrow = weights.astype(BF)
    slopes = (weights * (nt(own[1, 0], g_grad) - g_dot)).astype(BF)
    dkv[0, 0] = nn(slopes, g_query) * scale
    dkv[1, 0] = nn(narrow, g_grad)
    g_out = nn(own[1, 0].T, narrow).T
    g_dq = (nn(own[0, 0].T, slopes) * scale).T
    query, grad = qd[0, 0], qd[1, 0]
    weights = jnp.exp2(nt(g_key, query) * scale2 - log_dot[0, 0:1, :])
    slopes = (weights * (nt(g_value, grad) - log_dot[0, 1:2, :])).astype(BF)
    g_dv = nn(weights.astype(BF), grad)
    g_dk = nn(slopes, query)
    tables = [table.astype(BF) for table in (g_out, g_dq, g_dk * scale, g_dv)]
    spread = nn(expand[...], jnp.concatenate(tables, axis=1)).astype(BF)
    width = own.shape[3]
    for part in range(sums.shape[0]):
        for number in range(4):
            sums[part, number, 0] = spread[
                part * slots : (part + 1) * slots, number * width : (number + 1) * width
            ]


def backward_kernel(
    scale, scale2, qd, left, own, right, rows, bias, log_dot, before, dq, dkv, keys, values, probs, slopes
):
    toks = own.shape[2]
    reach = 2 * HALF + TILE
    join((left, own, right), 0, keys)
    join((left, own, right), 1, values)
    key_t = keys[...].T
    g_key, g_value = rows[1, 0], rows[2, 0]
    weights = jnp.exp2(nt(g_key, qd[0, 0]) * scale2 - log_dot[0, 0:1, :])
    slope = (weights * (nt(g_value, qd[1, 0]) - log_dot[0, 1:2, :])).astype(BF)
    dq_t = nn(g_key.T, slope)
    for q_tile in range(toks // TILE):
        lanes = slice(q_tile * TILE, (q_tile + 1) * TILE)
        query = qd[0, 0, lanes, :]
        grad = qd[1, 0, lanes, :]
        log_sum = log_dot[0, 0:1, lanes]
        dot = log_dot[0, 1:2, lanes]
        for piece in range(reach // TILE):
            start = (q_tile + piece) * TILE
            span = slice(start, start + TILE)
            scores = nt(keys[span, :], query) * scale2 + wide(bias[span, :], TILE)
            if piece == 0:
                scores = band(scores, False)
            elif piece == reach // TILE - 1:
                scores = band(scores, True)
            weights = jnp.exp2(scores - log_sum)
            slopes[span, lanes] = (weights * (nt(values[span, :], grad) - dot)).astype(BF)
            if HALF <= start < HALF + toks:
                probs[start - HALF : start - HALF + TILE, lanes] = weights.astype(BF)
        span = slice(q_tile * TILE, q_tile * TILE + reach)
        acc = dq_t[:, lanes] + nn(key_t[:, span], slopes[span, lanes])
        dq[0, lanes, :] = (acc * scale).T
    dkv[0, 0] = before[0, 0] + nn(slopes[HALF : HALF + toks, :], qd[0, 0]) * scale
    dkv[1, 0] = before[1, 0] + nn(probs[...], qd[1, 0])


def rim_kernel(
    scale, scale2, own, bias, qd_low, qd_high, log_low, log_high, partial, dkv, queries, grads, probs, slopes
):
    toks = own.shape[2]
    reach = toks + TILE
    join((qd_low, qd_high), 0, queries)
    join((qd_low, qd_high), 1, grads)
    for k_tile in range(toks // TILE):
        span = slice(k_tile * TILE, (k_tile + 1) * TILE)
        key = own[0, 0, span, :]
        value = own[1, 0, span, :]
        key_bias = wide(bias[HALF + k_tile * TILE : HALF + (k_tile + 1) * TILE, :], TILE)
        for piece in range(reach // TILE):
            start = (k_tile + piece) * TILE
            log_dot, offset = (log_low, start) if start < toks else (log_high, start - toks)
            lanes = slice(offset, offset + TILE)
            scores = nt(key, queries[start : start + TILE, :]) * scale2 + key_bias
            if piece == 0:
                scores = band(scores, True)
            elif piece == reach // TILE - 1:
                scores = band(scores, False)
            weights = jnp.exp2(scores - log_dot[0, 0:1, lanes])
            slope = weights * (nt(value, grads[start : start + TILE, :]) - log_dot[0, 1:2, lanes])
            spot = slice(piece * TILE, (piece + 1) * TILE)
            probs[span, spot] = weights.astype(BF)
            slopes[span, spot] = slope.astype(BF)
        window = slice(k_tile * TILE, k_tile * TILE + reach)
        dkv[0, 0, span, :] = partial[0, 0, span, :] + nn(slopes[span, :], queries[window, :]) * scale
        dkv[1, 0, span, :] = partial[1, 0, span, :] + nn(probs[span, :], grads[window, :])


def final_kernel(place, out, dq, dkv, sums, attn, query_grad, key_grad, value_grad, wide_rows):
    heads, toks = out.shape[0], out.shape[1]
    hot = place[...]
    is_global = jnp.sum(hot.astype(F32), axis=1, keepdims=True) > 0
    for head in range(heads):
        rows = pl.ds(head, toks, stride=heads)
        wide_rows[rows, :] = jnp.where(is_global, nn(hot, sums[0, head]), out[head].astype(F32))
        query_grad[rows, :] = dq[head] + nn(hot, sums[1, head])
        key_grad[rows, :] = dkv[0, head] + nn(hot, sums[2, head])
        value_grad[rows, :] = dkv[1, head] + nn(hot, sums[3, head])
    attn[...] = wide_rows[...].astype(BF)


def cost(flops, moved, exps=0):
    return pl.CostEstimate(flops=int(flops), bytes_accessed=int(moved), transcendentals=int(exps))


def struct(shape, dtype):
    return jax.ShapeDtypeStruct(shape, dtype)


def whole(shape):
    return pl.BlockSpec(shape, lambda head: (0,) * len(shape))


def per_head(shape, dim):
    block = tuple(1 if i == dim else size for i, size in enumerate(shape))
    return pl.BlockSpec(block, lambda head: tuple(head if i == dim else 0 for i in range(len(shape))))


def shards(query_rows, key_rows, value_rows, out_grad, global_pos):
    toks, heads, width = query_rows.shape
    count = global_pos.shape[0]
    devices = lax.axis_size("ctx")
    slots = max(16, 2 * count // devices)
    scale = width ** (-0.5)
    scale2 = scale * LOG2E
    bits = devices.bit_length() - 1
    ways = [list(range(1, bits)) + [0], list(range(bits - 1, 0, -1)) + [0]]
    orders = []
    for way in ways:
        order = [0]
        for bit in way[:-1]:
            order = order + [one | (1 << bit) for one in order]
        orders.append(order)
    orders = [mine + [one | 1 for one in other] for mine, other in (orders, orders[::-1])]
    pos_row = global_pos.reshape(1, count)
    q_flat, k_flat, v_flat, g_flat = (
        x.reshape(toks * heads, width) for x in (query_rows, key_rows, value_rows, out_grad)
    )

    def swap(value, stage):
        pairs = [(i, i ^ (1 << ways[i % 2][stage])) for i in range(devices)]
        return lax.ppermute(value, "ctx", pairs)

    def from_low(value):
        return lax.ppermute(value, "ctx", [(i, i + 1) for i in range(devices - 1)])

    def from_high(value):
        return lax.ppermute(value, "ctx", [(i + 1, i) for i in range(devices - 1)])

    def after(value, earlier):
        return lax.optimization_barrier((value, earlier))[0]

    pair_shape = (2, heads, toks, width)
    slot_shape = (4, heads, slots, width)
    steps = 1
    flat_spec = pl.BlockSpec((toks * heads // steps, width), lambda i: (i, 0))
    pair_spec = pl.BlockSpec((2, heads, toks // steps, width), lambda i: (0, 0, i, 0))
    wide_pair = pltpu.VMEM((2, toks * heads // steps, width), F32)
    kv = pl.pallas_call(
        functools.partial(pack_keys_kernel, heads),
        grid=(steps,),
        in_specs=[flat_spec, flat_spec],
        out_specs=pair_spec,
        out_shape=struct(pair_shape, BF),
        scratch_shapes=[wide_pair],
        compiler_params=params(),
        name="pack_keys",
    )(k_flat, v_flat)
    kv_low, kv_high = from_low(kv), from_high(kv)

    qd, slot_rows = pl.pallas_call(
        functools.partial(pack_queries_kernel, heads, slots),
        grid=(steps,),
        in_specs=[flat_spec, flat_spec, pair_spec, whole((1, count))],
        out_specs=(pair_spec, whole(slot_shape)),
        out_shape=(struct(pair_shape, BF), struct(slot_shape, BF)),
        scratch_shapes=[wide_pair, pltpu.VMEM(slot_shape, F32)],
        compiler_params=params(),
        name="pack_queries",
    )(q_flat, g_flat, kv, pos_row)

    held = [slot_rows[None]]
    for stage in range(bits):
        send = jnp.concatenate(held, axis=0) if len(held) > 1 else held[0]
        if stage == bits - 1:
            send = after(send, (kv_low, kv_high))
        held.append(swap(send, stage))
    qd_late = after(qd, (kv_low, kv_high))
    qd_low, qd_high = from_low(qd_late), from_high(qd_late)

    span = toks + 2 * HALF
    bias, bias_row, compact, expand, place = pl.pallas_call(
        functools.partial(mask_kernel, orders, slots, toks * devices),
        out_shape=(
            struct((span, 128), F32),
            struct((8, span), F32),
            struct((count, devices * slots), BF),
            struct((devices * slots, count), BF),
            struct((toks, slots), BF),
        ),
        compiler_params=params(),
        name="masks",
    )(pos_row)

    row_shape = (4, heads, count, width)
    rows, stats = pl.pallas_call(
        functools.partial(stats_kernel, scale2),
        grid=(heads,),
        in_specs=[whole(compact.shape)]
        + [per_head(part.shape, 2) for part in held]
        + [per_head(pair_shape, 1)],
        out_specs=(per_head(row_shape, 1), per_head((1, heads, 3, count), 1)),
        out_shape=(struct(row_shape, BF), struct((1, heads, 3, count), F32)),
        compiler_params=params(),
        cost_estimate=cost(2.7e9, 4e6),
        name="global_stats",
    )(compact, *held, kv)

    for stage in range(bits):
        stats = jnp.concatenate([stats, swap(stats, stage)], axis=0)

    head_specs = [
        per_head(pair_shape, 1),
        per_head(pair_shape, 1),
        per_head(pair_shape, 1),
        per_head(pair_shape, 1),
        per_head(row_shape, 1),
    ]
    out, log_dot = pl.pallas_call(
        functools.partial(forward_kernel, scale2),
        grid=(heads,),
        in_specs=head_specs + [whole(bias_row.shape)],
        out_specs=(per_head((heads, toks, width), 0), per_head((heads, 2, toks), 0)),
        out_shape=(struct((heads, toks, width), BF), struct((heads, 2, toks), F32)),
        scratch_shapes=[
            pltpu.VMEM((span, width), BF),
            pltpu.VMEM((span, width), BF),
            pltpu.VMEM((TILE, 2 * HALF + TILE + count), F32),
            pltpu.VMEM((TILE, 2 * HALF + TILE + count), BF),
        ],
        compiler_params=params(),
        cost_estimate=cost(4e9, 5e6, 3e6),
        name="forward",
    )(qd, kv_low, kv, kv_high, rows, bias_row)
    log_low, log_high = from_low(log_dot), from_high(log_dot)

    sum_shape = (devices, 4, heads, slots, width)
    dkv, sums = pl.pallas_call(
        functools.partial(global_kernel, scale, scale2, slots),
        grid=(heads,),
        in_specs=[
            per_head(pair_shape, 1),
            per_head(pair_shape, 1),
            per_head(row_shape, 1),
            per_head(log_dot.shape, 0),
            per_head(stats.shape, 1),
            whole(expand.shape),
        ],
        out_specs=(per_head(pair_shape, 1), per_head(sum_shape, 2)),
        out_shape=(struct(pair_shape, F32), struct(sum_shape, BF)),
        compiler_params=params(),
        cost_estimate=cost(4e9, 9e6, 1e6),
        name="globals",
    )(qd, kv, rows, log_dot, stats, expand)

    for stage in reversed(range(bits)):
        half = sums.shape[0] // 2
        sums = sums[:half] + swap(sums[half:], stage)

    dq, dkv = pl.pallas_call(
        functools.partial(backward_kernel, scale, scale2),
        grid=(heads,),
        in_specs=head_specs
        + [whole(bias.shape), per_head(log_dot.shape, 0), per_head(pair_shape, 1)],
        out_specs=(per_head((heads, toks, width), 0), per_head(pair_shape, 1)),
        out_shape=(struct((heads, toks, width), F32), struct(pair_shape, F32)),
        scratch_shapes=[
            pltpu.VMEM((span, width), BF),
            pltpu.VMEM((span, width), BF),
            pltpu.VMEM((toks, toks), BF),
            pltpu.VMEM((span, toks), BF),
        ],
        compiler_params=params(),
        cost_estimate=cost(8e9, 9e6, 3e6),
        name="backward",
    )(qd, kv_low, kv, kv_high, rows, bias, after(log_dot, (qd_low, qd_high)), dkv)

    dkv = pl.pallas_call(
        functools.partial(rim_kernel, scale, scale2),
        grid=(heads,),
        in_specs=[
            per_head(pair_shape, 1),
            whole(bias.shape),
            per_head(pair_shape, 1),
            per_head(pair_shape, 1),
            per_head(log_dot.shape, 0),
            per_head(log_dot.shape, 0),
            per_head(pair_shape, 1),
        ],
        out_specs=per_head(pair_shape, 1),
        out_shape=struct(pair_shape, F32),
        scratch_shapes=[
            pltpu.VMEM((2 * toks, width), BF),
            pltpu.VMEM((2 * toks, width), BF),
            pltpu.VMEM((toks, toks + TILE), BF),
            pltpu.VMEM((toks, toks + TILE), BF),
        ],
        compiler_params=params(),
        cost_estimate=cost(4e9, 8e6, 2e6),
        name="rim",
    )(kv, bias, qd_low, qd_high, log_low, log_high, dkv)

    flat_shape = (toks * heads, width)
    steps = 2
    outs = pl.pallas_call(
        final_kernel,
        grid=(steps,),
        in_specs=[
            pl.BlockSpec((toks // steps, slots), lambda i: (i, 0)),
            pl.BlockSpec((heads, toks // steps, width), lambda i: (0, i, 0)),
            pl.BlockSpec((heads, toks // steps, width), lambda i: (0, i, 0)),
            pl.BlockSpec((2, heads, toks // steps, width), lambda i: (0, 0, i, 0)),
            whole(slot_shape),
        ],
        out_specs=[pl.BlockSpec((toks * heads // steps, width), lambda i: (i, 0))] * 4,
        out_shape=[struct(flat_shape, kind) for kind in (BF, F32, F32, F32)],
        scratch_shapes=[pltpu.VMEM((toks * heads // steps, width), F32)],
        compiler_params=params(),
        name="final",
    )(place, out, dq, dkv, sums[0])
    return tuple(x.reshape(toks, heads, width) for x in outs)


def solution(mesh):
    spec = P("ctx", "head", None)
    return jax.shard_map(
        shards,
        mesh=mesh,
        in_specs=(spec, spec, spec, spec, P()),
        out_specs=(spec, spec, spec, spec),
        check_vma=False,
    )
```

profile of v0, /device:TPU:0, one launch (start us, length us, event | category | flops | bytes accessed | tf_op | source)
XLA Modules:
  0.0 118.6 jit_solution(14602920403973899576)
XLA Ops:
  0.6 2.4 %pack_keys.1.kv.refs_4_.own = bf16[2,4,512,128]{3,2,1,0:T(8,128)(2,1)} custom-call(bf16[2048,128]{1,0:T(8,128)(2,1)} %bitcast.16, bf16[2048,128]{1,0:T(8,128)(2,1)} %bitcast.17), custom_call_target="tpu_custom_call" | custom-call | tf_op jit(solution)/shard_map/pack_keys/pallas_call | solution.py:369
  3.1 3.4 %pack_queries.1 = (bf16[2,4,512,128]{3,2,1,0:T(8,128)(2,1)}, bf16[4,4,64,128]{3,2,1,0:T(8,128)(2,1)}) custom-call(bf16[2048,128]{1,0:T(8,128)(2,1)} %bitcast.18, bf16[2048,128]{1,0:T(8,128)(2,1)} %bitcast.19, bf16[2,4,512,128]{3,2,1,0:T(8,128)(2,1)} %pack_keys.1.kv.refs_4_.own, s32[1,256]{1,0:T(1,128)} %bitcast.20), custom_call_target="tpu_custom_call" | custom-call | tf_op jit(solution)/shard_map/pack_queries/pallas_call | solution.py:381
  6.5 2.9 %collective-permute-start.2 = (bf16[1,4,4,64,128]{4,3,2,1,0:T(8,128)(2,1)}, bf16[1,4,4,64,128]{4,3,2,1,0:T(8,128)(2,1)S(1)}, u32[]{:S(2)}, u32[]{:S(2)}) collective-permute-start(bf16[1,4,4,64,128]{4,3,2,1,0:T(8,128)(2,1)} %bitcast.12), channel_id=1, source_target_pairs={{0,8},{4,20},{8,0},{12,28},{16,24},{20,4},{24,16},{28,12},{1,9},{5... | collective-permute-start | bytes 786440 | tf_op jit(solution)/shard_map/ppermute | solution.py:352
  9.4 2.5 %collective-permute-start = (bf16[2,4,512,128]{3,2,1,0:T(8,128)(2,1)}, bf16[2,4,512,128]{3,2,1,0:T(8,128)(2,1)}, u32[]{:S(2)}, u32[]{:S(2)}) collective-permute-start(bf16[2,4,512,128]{3,2,1,0:T(8,128)(2,1)} %pack_keys.1.kv.refs_4_.own), channel_id=1, source_target_pairs={{0,4},{4,8},{8,12},{12,16},{16,20},{20,24},{24,28},{1,5},{5,9},{9,... | collective-permute-start | bytes 3145736 | tf_op jit(solution)/shard_map/ppermute | solution.py:355
  11.9 1.3 %collective-permute-start.1 = (bf16[2,4,512,128]{3,2,1,0:T(8,128)(2,1)}, bf16[2,4,512,128]{3,2,1,0:T(8,128)(2,1)}, u32[]{:S(2)}, u32[]{:S(2)}) collective-permute-start(bf16[2,4,512,128]{3,2,1,0:T(8,128)(2,1)} %pack_keys.1.kv.refs_4_.own), channel_id=1, source_target_pairs={{4,0},{8,4},{12,8},{16,12},{20,16},{24,20},{28,24},{5,1},{9,5},{13... | collective-permute-start | bytes 3145736 | tf_op jit(solution)/shard_map/ppermute | solution.py:358
  13.2 1.9 %collective-permute-done.2.refs_1_ = bf16[1,4,4,64,128]{4,3,2,1,0:T(8,128)(2,1)S(1)} collective-permute-done((bf16[1,4,4,64,128]{4,3,2,1,0:T(8,128)(2,1)}, bf16[1,4,4,64,128]{4,3,2,1,0:T(8,128)(2,1)S(1)}, u32[]{:S(2)}, u32[]{:S(2)}) %collective-permute-start.2) | collective-permute-done | bytes 262176 | tf_op jit(solution)/shard_map/ppermute | solution.py:352
  15.1 1.1 pad_maximum_fusion.1
  16.2 2.4 %collective-permute-start.3 = (bf16[2,4,4,64,128]{4,3,2,1,0:T(8,128)(2,1)S(1)}, bf16[2,4,4,64,128]{4,3,2,1,0:T(8,128)(2,1)S(1)}, u32[]{:S(2)}, u32[]{:S(2)}) collective-permute-start(bf16[2,4,4,64,128]{4,3,2,1,0:T(8,128)(2,1)S(1)} %pad_maximum_fusion.1), channel_id=1, source_target_pairs={{0,16},{4,12},{8,24},{12,4},{16,0},{20,28},{24,8},{28,20},{1,17},{... | collective-permute-start | bytes 1572872 | tf_op jit(solution)/shard_map/ppermute | solution.py:352
  18.6 12.2 %collective-permute-done.3.refs_2_ = bf16[2,4,4,64,128]{4,3,2,1,0:T(8,128)(2,1)S(1)} collective-permute-done((bf16[2,4,4,64,128]{4,3,2,1,0:T(8,128)(2,1)S(1)}, bf16[2,4,4,64,128]{4,3,2,1,0:T(8,128)(2,1)S(1)}, u32[]{:S(2)}, u32[]{:S(2)}) %collective-permute-start.3) | collective-permute-done | bytes 524320 | tf_op jit(solution)/shard_map/ppermute | solution.py:352
  30.8 2.2 %pad_maximum_fusion = bf16[4,4,4,64,128]{4,3,2,1,0:T(8,128)(2,1)} fusion(bf16[2,4,4,64,128]{4,3,2,1,0:T(8,128)(2,1)S(1)} %collective-permute-done.3.refs_2_, bf16[1,4,4,64,128]{4,3,2,1,0:T(8,128)(2,1)S(1)} %collective-permute-done.2.refs_1_, bf16[1,4,4,64,128]{4,3,2,1,0:T(8,128)(2,1)} %bitcast.14), kind=kLoop, calls=%fused_computation | loop fusion | flops 1048576 | bytes 2097152 | tf_op jit(solution)/shard_map/concatenate | solution.py:394
  33.0 0.0 collective-permute-done.left
  33.0 0.0 collective-permute-done.1.right
  33.0 12.6 %collective-permute-start.4 = (bf16[4,4,4,64,128]{4,3,2,1,0:T(8,128)(2,1)}, bf16[4,4,4,64,128]{4,3,2,1,0:T(8,128)(2,1)}, u32[]{:S(2)}, u32[]{:S(2)}) collective-permute-start(bf16[4,4,4,64,128]{4,3,2,1,0:T(8,128)(2,1)} %pad_maximum_fusion), channel_id=1, source_target_pairs={{0,4},{4,0},{8,12},{12,8},{16,20},{20,16},{24,28},{28,24},{1,5},{5... | collective-permute-start | bytes 3145736 | tf_op jit(solution)/shard_map/ppermute | solution.py:352
  45.6 2.7 %masks.1 = (f32[1536,128]{1,0:T(8,128)}, f32[8,1536]{1,0:T(8,128)}, bf16[256,512]{1,0:T(8,128)(2,1)}, bf16[512,256]{1,0:T(8,128)(2,1)}, bf16[512,64]{1,0:T(8,128)(2,1)}) custom-call(s32[1,256]{1,0:T(1,128)} %bitcast.21), custom_call_target="tpu_custom_call" | custom-call | tf_op jit(solution)/shard_map/masks/pallas_call | solution.py:402
  48.3 0.0 collective-permute-done.4.refs_3_
  48.3 5.5 %global_stats.1 = (bf16[4,4,256,128]{3,2,1,0:T(8,128)(2,1)}, f32[1,4,3,256]{3,2,1,0:T(4,128)}) custom-call(bf16[256,512]{1,0:T(8,128)(2,1)} %get-tuple-element.28.compact, bf16[1,4,4,64,128]{4,3,2,1,0:T(8,128)(2,1)} %bitcast.15, bf16[1,4,4,64,128]{4,3,2,1,0:T(8,128)(2,1)} %copy-done.2, bf16[2,4,4,64,128]{4,3,2,1,0:T(8,128)(2,1)} %copy-done.3, ...), custom_call_target="tpu_custom_call" | custom-call | flops 2700000000 | bytes 4000000 | tf_op jit(solution)/shard_map/global_stats/pallas_call | solution.py:416
  53.7 0.0 collective-permute-start.7
  53.7 3.9 %collective-permute-done.7 = f32[1,4,3,256]{3,2,1,0:T(4,128)S(1)} collective-permute-done((f32[1,4,3,256]{3,2,1,0:T(4,128)}, f32[1,4,3,256]{3,2,1,0:T(4,128)S(1)}, u32[]{:S(2)}, u32[]{:S(2)}) %collective-permute-start.7) | collective-permute-done | bytes 12320 | tf_op jit(solution)/shard_map/ppermute | solution.py:352
  57.7 0.7 pad_maximum_fusion.4
  58.4 0.1 collective-permute-start.8
  58.5 2.2 %collective-permute-start.5 = (bf16[2,4,512,128]{3,2,1,0:T(8,128)(2,1)}, bf16[2,4,512,128]{3,2,1,0:T(8,128)(2,1)}, u32[]{:S(2)}, u32[]{:S(2)}) collective-permute-start(bf16[2,4,512,128]{3,2,1,0:T(8,128)(2,1)} %get-tuple-element.36.qd), channel_id=1, source_target_pairs={{0,4},{4,8},{8,12},{12,16},{16,20},{20,24},{24,28},{1,5},{5,9},{9,... | collective-permute-start | bytes 3145736 | tf_op jit(solution)/shard_map/ppermute | solution.py:355
  60.8 1.3 %collective-permute-start.6 = (bf16[2,4,512,128]{3,2,1,0:T(8,128)(2,1)}, bf16[2,4,512,128]{3,2,1,0:T(8,128)(2,1)}, u32[]{:S(2)}, u32[]{:S(2)}) collective-permute-start(bf16[2,4,512,128]{3,2,1,0:T(8,128)(2,1)} %get-tuple-element.36.qd), channel_id=1, source_target_pairs={{4,0},{8,4},{12,8},{16,12},{20,16},{24,20},{28,24},{5,1},{9,5},{13... | collective-permute-start | bytes 3145736 | tf_op jit(solution)/shard_map/ppermute | solution.py:358
  62.1 0.3 collective-permute-done.8
  62.4 0.7 pad_maximum_fusion.3
  63.1 2.2 %collective-permute-start.9 = (f32[4,4,3,256]{3,2,1,0:T(4,128)S(1)}, f32[4,4,3,256]{3,2,1,0:T(4,128)S(1)}, u32[]{:S(2)}, u32[]{:S(2)}) collective-permute-start(f32[4,4,3,256]{3,2,1,0:T(4,128)S(1)} %pad_maximum_fusion.3), channel_id=1, source_target_pairs={{0,4},{4,0},{8,12},{12,8},{16,20},{20,16},{24,28},{28,24},{1,5},{5... | collective-permute-start | bytes 147464 | tf_op jit(solution)/shard_map/ppermute | solution.py:352
  65.3 9.3 %forward.1 = (bf16[4,512,128]{2,1,0:T(8,128)(2,1)}, f32[4,2,512]{2,1,0:T(2,128)}) custom-call(bf16[2,4,512,128]{3,2,1,0:T(8,128)(2,1)} %get-tuple-element.36.qd, bf16[2,4,512,128]{3,2,1,0:T(8,128)(2,1)} %collective-permute-done.left, bf16[2,4,512,128]{3,2,1,0:T(8,128)(2,1)} %pack_keys.1.kv.refs_4_.own, ...), custom_call_target="tpu_custom_call" | custom-call | flops 4000000000 | bytes 5000000 | tf_op jit(solution)/shard_map/forward/pallas_call | solution.py:439
  74.7 0.7 pad_maximum_fusion.2.stats
  75.4 7.0 %globals.1 = (f32[2,4,512,128]{3,2,1,0:T(8,128)}, bf16[8,4,4,64,128]{4,3,2,1,0:T(8,128)(2,1)}) custom-call(bf16[2,4,512,128]{3,2,1,0:T(8,128)(2,1)} %get-tuple-element.36.qd, bf16[2,4,512,128]{3,2,1,0:T(8,128)(2,1)} %pack_keys.1.kv.refs_4_.own, bf16[4,4,256,128]{3,2,1,0:T(8,128)(2,1)} %get-tuple-element.31.rows, f32[4,2,512]{2,1,0:T(2,128)} %get-tuple-element.37.log_dot, ...), custom_call_target="tpu_custom_call" | custom-call | flops 4000000000 | bytes 9000000 | tf_op jit(solution)/shard_map/globals/pallas_call | solution.py:458
  82.4 1.5 %slice.19 = bf16[4,4,4,64,128]{4,3,2,1,0:T(8,128)(2,1)S(1)} slice(bf16[8,4,4,64,128]{4,3,2,1,0:T(8,128)(2,1)} %get-tuple-element.43), slice={[4:8], [0:4], [0:4], [0:64], [0:128]} | slice | bytes 2097152 | tf_op jit(solution)/shard_map/slice | solution.py:478
  83.9 0.1 collective-permute-start.12
  83.9 2.4 %collective-permute-start.10 = (f32[4,2,512]{2,1,0:T(2,128)S(1)}, f32[4,2,512]{2,1,0:T(2,128)S(1)}, u32[]{:S(2)}, u32[]{:S(2)}) collective-permute-start(f32[4,2,512]{2,1,0:T(2,128)S(1)} %copy-done.5), channel_id=1, source_target_pairs={{0,4},{4,8},{8,12},{12,16},{16,20},{20,24},{24,28},{1,5},{5,9},{9,... | collective-permute-start | bytes 49160 | tf_op jit(solution)/shard_map/ppermute | solution.py:355
  86.3 1.3 %collective-permute-start.11 = (f32[4,2,512]{2,1,0:T(2,128)S(1)}, f32[4,2,512]{2,1,0:T(2,128)S(1)}, u32[]{:S(2)}, u32[]{:S(2)}) collective-permute-start(f32[4,2,512]{2,1,0:T(2,128)S(1)} %copy-done.5), channel_id=1, source_target_pairs={{4,0},{8,4},{12,8},{16,12},{20,16},{24,20},{28,24},{5,1},{9,5},{13... | collective-permute-start | bytes 49160 | tf_op jit(solution)/shard_map/ppermute | solution.py:358
  87.6 0.0 collective-permute-done.5.qd_low
  87.6 0.0 collective-permute-done.6.qd_high
  87.7 0.1 slice_add_fusion
  87.8 1.0 copy-done
  88.8 5.8 %collective-permute-start.13 = (bf16[2,4,4,64,128]{4,3,2,1,0:T(8,128)(2,1)S(1)}, bf16[2,4,4,64,128]{4,3,2,1,0:T(8,128)(2,1)}, u32[]{:S(2)}, u32[]{:S(2)}) collective-permute-start(bf16[2,4,4,64,128]{4,3,2,1,0:T(8,128)(2,1)S(1)} %slice.25), channel_id=1, source_target_pairs={{0,16},{4,12},{8,24},{12,4},{16,0},{20,28},{24,8},{28,20},{1,17},{... | collective-permute-start | bytes 1572872 | tf_op jit(solution)/shard_map/ppermute | solution.py:352
  94.6 9.6 %backward.1 = (f32[4,512,128]{2,1,0:T(8,128)}, f32[2,4,512,128]{3,2,1,0:T(8,128)}) custom-call(bf16[2,4,512,128]{3,2,1,0:T(8,128)(2,1)} %get-tuple-element.36.qd, bf16[2,4,512,128]{3,2,1,0:T(8,128)(2,1)} %collective-permute-done.left, bf16[2,4,512,128]{3,2,1,0:T(8,128)(2,1)} %pack_keys.1.kv.refs_4_.own, ...), custom_call_target="tpu_custom_call" | custom-call | flops 8000000000 | bytes 9000000 | tf_op jit(solution)/shard_map/backward/pallas_call | solution.py:480
  104.3 1.3 %slice_add_fusion.1 = bf16[2,4,4,64,128]{4,3,2,1,0:T(8,128)(2,1)S(1)} fusion(bf16[2,4,4,64,128]{4,3,2,1,0:T(8,128)(2,1)} %collective-permute-done.13, bf16[4,4,4,64,128]{4,3,2,1,0:T(8,128)(2,1)} %copy-done), kind=kLoop, calls=%fused_computation.2 | loop fusion | flops 262144 | bytes 1572864 | tf_op jit(solution)/shard_map/add | solution.py:478
  105.5 0.7 slice.27
  106.2 0.0 collective-permute-start.14
  106.2 0.0 collective-permute-done.10.log_low
  106.3 0.0 copy-start.7
  106.3 0.6 copy-done.6
  106.8 0.0 copy-done.7
  106.9 7.1 %rim.1.dkv = f32[2,4,512,128]{3,2,1,0:T(8,128)} custom-call(bf16[2,4,512,128]{3,2,1,0:T(8,128)(2,1)} %pack_keys.1.kv.refs_4_.own, f32[1536,128]{1,0:T(8,128)} %get-tuple-element.34.bias, bf16[2,4,512,128]{3,2,1,0:T(8,128)(2,1)} %collective-permute-done.5.qd_low, bf16[2,4,512,128]{3,2,1,0:T(8,128)(2,1)} %collective-permute-done.6.qd_high, ...), custom_call_target="tpu_custom_call" | custom-call | flops 4000000000 | bytes 8000000 | tf_op jit(solution)/shard_map/rim/pallas_call | solution.py:498
  114.0 0.7 fusion.sums
  114.7 3.9 %final.1 = (bf16[2048,128]{1,0:T(8,128)(2,1)}, f32[2048,128]{1,0:T(8,128)}, f32[2048,128]{1,0:T(8,128)}, f32[2048,128]{1,0:T(8,128)}) custom-call(bf16[512,64]{1,0:T(8,128)(2,1)} %get-tuple-element.26.place, bf16[4,512,128]{2,1,0:T(8,128)(2,1)} %get-tuple-element.33.out, f32[4,512,128]{2,1,0:T(8,128)} %get-tuple-element.41.dq, f32[2,4,512,128]{3,2,1,0:T(8,128)} %rim.1.dkv, ...), custom_call_target="tpu_custom_call" | custom-call | tf_op jit(solution)/shard_map/final/pallas_call | solution.py:525
  (18 shorter events, 0.1 us)
Async XLA Ops:
  6.5 8.6 %collective-permute-start.2 = (bf16[1,4,4,64,128]{4,3,2,1,0:T(8,128)(2,1)}, bf16[1,4,4,64,128]{4,3,2,1,0:T(8,128)(2,1)S(1)}, u32[]{:S(2)}, u32[]{:S(2)}) collective-permute-start(bf16[1,4,4,64,128]{4,3,2,1,0:T(8,128)(2,1)} %bitcast.12), channel_id=1, source_target_pairs={{0,8},{4,20},{8,0},{12,28},{16,24},{20,4},{24,16},{28,12},{1,9},{5... | collective-permute-start | bytes 786440 | tf_op jit(solution)/shard_map/ppermute | solution.py:352
  9.4 23.5 %collective-permute-start = (bf16[2,4,512,128]{3,2,1,0:T(8,128)(2,1)}, bf16[2,4,512,128]{3,2,1,0:T(8,128)(2,1)}, u32[]{:S(2)}, u32[]{:S(2)}) collective-permute-start(bf16[2,4,512,128]{3,2,1,0:T(8,128)(2,1)} %pack_keys.1.kv.refs_4_.own), channel_id=1, source_target_pairs={{0,4},{4,8},{8,12},{12,16},{16,20},{20,24},{24,28},{1,5},{5,9},{9,... | collective-permute-start | bytes 3145736 | tf_op jit(solution)/shard_map/ppermute | solution.py:355
  11.9 21.0 %collective-permute-start.1 = (bf16[2,4,512,128]{3,2,1,0:T(8,128)(2,1)}, bf16[2,4,512,128]{3,2,1,0:T(8,128)(2,1)}, u32[]{:S(2)}, u32[]{:S(2)}) collective-permute-start(bf16[2,4,512,128]{3,2,1,0:T(8,128)(2,1)} %pack_keys.1.kv.refs_4_.own), channel_id=1, source_target_pairs={{4,0},{8,4},{12,8},{16,12},{20,16},{24,20},{28,24},{5,1},{9,5},{13... | collective-permute-start | bytes 3145736 | tf_op jit(solution)/shard_map/ppermute | solution.py:358
  15.1 33.2 %copy-start.2 = (bf16[1,4,4,64,128]{4,3,2,1,0:T(8,128)(2,1)}, bf16[1,4,4,64,128]{4,3,2,1,0:T(8,128)(2,1)S(1)}, u32[]{:S(2)}) copy-start(bf16[1,4,4,64,128]{4,3,2,1,0:T(8,128)(2,1)S(1)} %collective-permute-done.2.refs_1_) | copy-start | bytes 786436
  16.2 14.6 %collective-permute-start.3 = (bf16[2,4,4,64,128]{4,3,2,1,0:T(8,128)(2,1)S(1)}, bf16[2,4,4,64,128]{4,3,2,1,0:T(8,128)(2,1)S(1)}, u32[]{:S(2)}, u32[]{:S(2)}) collective-permute-start(bf16[2,4,4,64,128]{4,3,2,1,0:T(8,128)(2,1)S(1)} %pad_maximum_fusion.1), channel_id=1, source_target_pairs={{0,16},{4,12},{8,24},{12,4},{16,0},{20,28},{24,8},{28,20},{1,17},{... | collective-permute-start | bytes 1572872 | tf_op jit(solution)/shard_map/ppermute | solution.py:352
  30.8 17.5 %copy-start.3 = (bf16[2,4,4,64,128]{4,3,2,1,0:T(8,128)(2,1)}, bf16[2,4,4,64,128]{4,3,2,1,0:T(8,128)(2,1)S(1)}, u32[]{:S(2)}) copy-start(bf16[2,4,4,64,128]{4,3,2,1,0:T(8,128)(2,1)S(1)} %collective-permute-done.3.refs_2_) | copy-start | bytes 1572868
  33.0 15.3 %collective-permute-start.4 = (bf16[4,4,4,64,128]{4,3,2,1,0:T(8,128)(2,1)}, bf16[4,4,4,64,128]{4,3,2,1,0:T(8,128)(2,1)}, u32[]{:S(2)}, u32[]{:S(2)}) collective-permute-start(bf16[4,4,4,64,128]{4,3,2,1,0:T(8,128)(2,1)} %pad_maximum_fusion), channel_id=1, source_target_pairs={{0,4},{4,0},{8,12},{12,8},{16,20},{20,16},{24,28},{28,24},{1,5},{5... | collective-permute-start | bytes 3145736 | tf_op jit(solution)/shard_map/ppermute | solution.py:352
  53.7 3.9 %collective-permute-start.7 = (f32[1,4,3,256]{3,2,1,0:T(4,128)}, f32[1,4,3,256]{3,2,1,0:T(4,128)S(1)}, u32[]{:S(2)}, u32[]{:S(2)}) collective-permute-start(f32[1,4,3,256]{3,2,1,0:T(4,128)} %get-tuple-element.38), channel_id=1, source_target_pairs={{0,8},{4,20},{8,0},{12,28},{16,24},{20,4},{24,16},{28,12},{1,9},{5... | collective-permute-start | bytes 36872 | tf_op jit(solution)/shard_map/ppermute | solution.py:352
  58.4 4.0 %collective-permute-start.8 = (f32[2,4,3,256]{3,2,1,0:T(4,128)S(1)}, f32[2,4,3,256]{3,2,1,0:T(4,128)S(1)}, u32[]{:S(2)}, u32[]{:S(2)}) collective-permute-start(f32[2,4,3,256]{3,2,1,0:T(4,128)S(1)} %pad_maximum_fusion.4), channel_id=1, source_target_pairs={{0,16},{4,12},{8,24},{12,4},{16,0},{20,28},{24,8},{28,20},{1,17},{... | collective-permute-start | bytes 73736 | tf_op jit(solution)/shard_map/ppermute | solution.py:352
  58.5 29.1 %collective-permute-start.5 = (bf16[2,4,512,128]{3,2,1,0:T(8,128)(2,1)}, bf16[2,4,512,128]{3,2,1,0:T(8,128)(2,1)}, u32[]{:S(2)}, u32[]{:S(2)}) collective-permute-start(bf16[2,4,512,128]{3,2,1,0:T(8,128)(2,1)} %get-tuple-element.36.qd), channel_id=1, source_target_pairs={{0,4},{4,8},{8,12},{12,16},{16,20},{20,24},{24,28},{1,5},{5,9},{9,... | collective-permute-start | bytes 3145736 | tf_op jit(solution)/shard_map/ppermute | solution.py:355
  60.8 26.9 %collective-permute-start.6 = (bf16[2,4,512,128]{3,2,1,0:T(8,128)(2,1)}, bf16[2,4,512,128]{3,2,1,0:T(8,128)(2,1)}, u32[]{:S(2)}, u32[]{:S(2)}) collective-permute-start(bf16[2,4,512,128]{3,2,1,0:T(8,128)(2,1)} %get-tuple-element.36.qd), channel_id=1, source_target_pairs={{4,0},{8,4},{12,8},{16,12},{20,16},{24,20},{28,24},{5,1},{9,5},{13... | collective-permute-start | bytes 3145736 | tf_op jit(solution)/shard_map/ppermute | solution.py:358
  63.1 11.5 %collective-permute-start.9 = (f32[4,4,3,256]{3,2,1,0:T(4,128)S(1)}, f32[4,4,3,256]{3,2,1,0:T(4,128)S(1)}, u32[]{:S(2)}, u32[]{:S(2)}) collective-permute-start(f32[4,4,3,256]{3,2,1,0:T(4,128)S(1)} %pad_maximum_fusion.3), channel_id=1, source_target_pairs={{0,4},{4,0},{8,12},{12,8},{16,20},{20,16},{24,28},{28,24},{1,5},{5... | collective-permute-start | bytes 147464 | tf_op jit(solution)/shard_map/ppermute | solution.py:352
  65.3 9.4 %copy-start.4 = (f32[1,4,3,256]{3,2,1,0:T(4,128)S(1)}, f32[1,4,3,256]{3,2,1,0:T(4,128)}, u32[]{:S(2)}) copy-start(f32[1,4,3,256]{3,2,1,0:T(4,128)} %get-tuple-element.38) | copy-start | bytes 36868
  75.4 8.6 %copy-start.5 = (f32[4,2,512]{2,1,0:T(2,128)S(1)}, f32[4,2,512]{2,1,0:T(2,128)}, u32[]{:S(2)}) copy-start(f32[4,2,512]{2,1,0:T(2,128)} %get-tuple-element.37.log_dot) | copy-start | bytes 49156
  82.4 5.3 %copy-start.1 = (bf16[8,4,4,64,128]{4,3,2,1,0:T(8,128)(2,1)S(1)}, bf16[8,4,4,64,128]{4,3,2,1,0:T(8,128)(2,1)}, u32[]{:S(2)}) copy-start(bf16[8,4,4,64,128]{4,3,2,1,0:T(8,128)(2,1)} %get-tuple-element.43) | copy-start | bytes 6291460
  83.9 3.8 %collective-permute-start.12 = (bf16[4,4,4,64,128]{4,3,2,1,0:T(8,128)(2,1)S(1)}, bf16[4,4,4,64,128]{4,3,2,1,0:T(8,128)(2,1)S(1)}, u32[]{:S(2)}, u32[]{:S(2)}) collective-permute-start(bf16[4,4,4,64,128]{4,3,2,1,0:T(8,128)(2,1)S(1)} %slice.19), channel_id=1, source_target_pairs={{0,4},{4,0},{8,12},{12,8},{16,20},{20,16},{24,28},{28,24},{1,5},{5... | collective-permute-start | bytes 3145736 | tf_op jit(solution)/shard_map/ppermute | solution.py:352
  83.9 22.3 %collective-permute-start.10 = (f32[4,2,512]{2,1,0:T(2,128)S(1)}, f32[4,2,512]{2,1,0:T(2,128)S(1)}, u32[]{:S(2)}, u32[]{:S(2)}) collective-permute-start(f32[4,2,512]{2,1,0:T(2,128)S(1)} %copy-done.5), channel_id=1, source_target_pairs={{0,4},{4,8},{8,12},{12,16},{16,20},{20,24},{24,28},{1,5},{5,9},{9,... | collective-permute-start | bytes 49160 | tf_op jit(solution)/shard_map/ppermute | solution.py:355
  86.3 19.9 %collective-permute-start.11 = (f32[4,2,512]{2,1,0:T(2,128)S(1)}, f32[4,2,512]{2,1,0:T(2,128)S(1)}, u32[]{:S(2)}, u32[]{:S(2)}) collective-permute-start(f32[4,2,512]{2,1,0:T(2,128)S(1)} %copy-done.5), channel_id=1, source_target_pairs={{4,0},{8,4},{12,8},{16,12},{20,16},{24,20},{28,24},{5,1},{9,5},{13... | collective-permute-start | bytes 49160 | tf_op jit(solution)/shard_map/ppermute | solution.py:358
  87.8 1.0 copy-start
  88.8 15.4 %collective-permute-start.13 = (bf16[2,4,4,64,128]{4,3,2,1,0:T(8,128)(2,1)S(1)}, bf16[2,4,4,64,128]{4,3,2,1,0:T(8,128)(2,1)}, u32[]{:S(2)}, u32[]{:S(2)}) collective-permute-start(bf16[2,4,4,64,128]{4,3,2,1,0:T(8,128)(2,1)S(1)} %slice.25), channel_id=1, source_target_pairs={{0,16},{4,12},{8,24},{12,4},{16,0},{20,28},{24,8},{28,20},{1,17},{... | collective-permute-start | bytes 1572872 | tf_op jit(solution)/shard_map/ppermute | solution.py:352
  106.2 7.8 %collective-permute-start.14 = (bf16[1,4,4,64,128]{4,3,2,1,0:T(8,128)(2,1)}, bf16[1,4,4,64,128]{4,3,2,1,0:T(8,128)(2,1)S(1)}, u32[]{:S(2)}, u32[]{:S(2)}) collective-permute-start(bf16[1,4,4,64,128]{4,3,2,1,0:T(8,128)(2,1)} %slice.27), channel_id=1, source_target_pairs={{0,8},{4,20},{8,0},{12,28},{16,24},{20,4},{24,16},{28,12},{1,9},{5... | collective-permute-start | bytes 786440 | tf_op jit(solution)/shard_map/ppermute | solution.py:352
  106.2 0.6 copy-start.6
  106.3 0.6 copy-start.7
where the time goes:
time: 119 us
  Pallas kernels  51 us (43%)
  starting transfers between devices  37.1 us (31%)
  waiting for transfers between devices  18.4 us (15%)
  other arithmetic  7.52 us (6%)
  local copies, waits for them, and re-layouts  3.84 us (3%)
    ppermute x9, starting transfers between devices, swap(): return lax.ppermute(value, 'ctx', pairs)  26.2 us
    ppermute x9, waiting for transfers between devices, swap(): return lax.ppermute(value, 'ctx', pairs)  18.3 us
    pallas_call x1, Pallas kernels, shards(): pl.pallas_call(functools.partial(backward_kernel, scale, scale2), grid=(h...  9.6 us
    pallas_call x1, Pallas kernels, shards(): pl.pallas_call(functools.partial(forward_kernel, scale2), grid=(heads,),...  9.35 us
    pallas_call x1, Pallas kernels, shards(): pl.pallas_call(functools.partial(rim_kernel, scale, scale2), grid=(heads,...  7.12 us
    ppermute x3, starting transfers between devices, from_low(): return lax.ppermute(value, 'ctx', [(i, i + 1) for i in range(devices - 1)])  7.11 us
    pallas_call x1, Pallas kernels, shards(): pl.pallas_call(functools.partial(global_kernel, scale, scale2, slots), gr...  7.02 us
    pallas_call x1, Pallas kernels, shards(): pl.pallas_call(functools.partial(stats_kernel, scale2), grid=(heads,), in...  5.45 us
  transfers between devices with their start and end apart: 15, of which 4 were waited for; matrix products, arithmetic and copies ran while one was open for 7% of the time, Pallas kernels for 30%

commit v1 on v0

--- a/solution.py
+++ b/solution.py
@@ -197,7 +197,7 @@
         log_dot[0, :, lanes] = pair.T[0:2, :]
 
 
-def global_kernel(scale, scale2, slots, qd, own, rows, log_dot, stats, expand, dkv, sums):
+def global_kernel(scale, scale2, slots, qd, own, rows, log_dot, stats, expand, dkv, kept, sent):
     toks = own.shape[2]
     g_query, g_key, g_value, g_grad = (rows[i, 0] for i in range(4))
     tops = stats[:, 0, 0:1, :]
@@ -221,9 +221,11 @@
     tables = [table.astype(BF) for table in (g_out, g_dq, g_dk * scale, g_dv)]
     spread = nn(expand[...], jnp.concatenate(tables, axis=1)).astype(BF)
     width = own.shape[3]
-    for part in range(sums.shape[0]):
+    half = kept.shape[0]
+    for part in range(2 * half):
+        sums = kept if part < half else sent
         for number in range(4):
-            sums[part, number, 0] = spread[
+            sums[part % half, number, 0] = spread[
                 part * slots : (part + 1) * slots, number * width : (number + 1) * width
             ]
 
@@ -296,16 +298,20 @@
         dkv[1, 0, span, :] = partial[1, 0, span, :] + nn(probs[span, :], grads[window, :])
 
 
-def final_kernel(place, out, dq, dkv, sums, attn, query_grad, key_grad, value_grad, wide_rows):
+def final_kernel(halves, place, out, sums, *refs):
+    dqs, pairs = refs[:halves], refs[halves : 2 * halves]
+    attn, query_grad, key_grad, value_grad, wide_rows = refs[2 * halves :]
     heads, toks = out.shape[0], out.shape[1]
+    group = heads // halves
     hot = place[...]
     is_global = jnp.sum(hot.astype(F32), axis=1, keepdims=True) > 0
     for head in range(heads):
+        dq, pair, part = dqs[head // group], pairs[head // group], head % group
         rows = pl.ds(head, toks, stride=heads)
         wide_rows[rows, :] = jnp.where(is_global, nn(hot, sums[0, head]), out[head].astype(F32))
-        query_grad[rows, :] = dq[head] + nn(hot, sums[1, head])
-        key_grad[rows, :] = dkv[0, head] + nn(hot, sums[2, head])
-        value_grad[rows, :] = dkv[1, head] + nn(hot, sums[3, head])
+        query_grad[rows, :] = dq[part] + nn(hot, sums[1, head])
+        key_grad[rows, :] = pair[0, part] + nn(hot, sums[2, head])
+        value_grad[rows, :] = pair[1, part] + nn(hot, sums[3, head])
     attn[...] = wide_rows[...].astype(BF)
 
 
@@ -321,9 +327,11 @@
     return pl.BlockSpec(shape, lambda head: (0,) * len(shape))
 
 
-def per_head(shape, dim):
+def per_head(shape, dim, first=0):
     block = tuple(1 if i == dim else size for i, size in enumerate(shape))
-    return pl.BlockSpec(block, lambda head: tuple(head if i == dim else 0 for i in range(len(shape))))
+    return pl.BlockSpec(
+        block, lambda head: tuple(head + first if i == dim else 0 for i in range(len(shape)))
+    )
 
 
 def shards(query_rows, key_rows, value_rows, out_grad, global_pos):
@@ -376,7 +384,6 @@
         compiler_params=params(),
         name="pack_keys",
     )(k_flat, v_flat)
-    kv_low, kv_high = from_low(kv), from_high(kv)
 
     qd, slot_rows = pl.pallas_call(
         functools.partial(pack_queries_kernel, heads, slots),
@@ -392,9 +399,9 @@
     held = [slot_rows[None]]
     for stage in range(bits):
         send = jnp.concatenate(held, axis=0) if len(held) > 1 else held[0]
-        if stage == bits - 1:
-            send = after(send, (kv_low, kv_high))
         held.append(swap(send, stage))
+    kv_late = after(kv, held[1])
+    kv_low, kv_high = from_low(kv_late), from_high(kv_late)
     qd_late = after(qd, (kv_low, kv_high))
     qd_low, qd_high = from_low(qd_late), from_high(qd_late)
 
@@ -454,8 +461,8 @@
     )(qd, kv_low, kv, kv_high, rows, bias_row)
     log_low, log_high = from_low(log_dot), from_high(log_dot)
 
-    sum_shape = (devices, 4, heads, slots, width)
-    dkv, sums = pl.pallas_call(
+    sum_shape = (devices // 2, 4, heads, slots, width)
+    dkv, sums, sent = pl.pallas_call(
         functools.partial(global_kernel, scale, scale2, slots),
         grid=(heads,),
         in_specs=[
@@ -466,78 +473,94 @@
             per_head(stats.shape, 1),
             whole(expand.shape),
         ],
-        out_specs=(per_head(pair_shape, 1), per_head(sum_shape, 2)),
-        out_shape=(struct(pair_shape, F32), struct(sum_shape, BF)),
+        out_specs=(per_head(pair_shape, 1), per_head(sum_shape, 2), per_head(sum_shape, 2)),
+        out_shape=(struct(pair_shape, F32), struct(sum_shape, BF), struct(sum_shape, BF)),
         compiler_params=params(),
         cost_estimate=cost(4e9, 9e6, 1e6),
         name="globals",
     )(qd, kv, rows, log_dot, stats, expand)
 
-    for stage in reversed(range(bits)):
+    sums = sums + swap(sent, bits - 1)
+    for stage in reversed(range(bits - 1)):
         half = sums.shape[0] // 2
         sums = sums[:half] + swap(sums[half:], stage)
 
-    dq, dkv = pl.pallas_call(
-        functools.partial(backward_kernel, scale, scale2),
-        grid=(heads,),
-        in_specs=head_specs
-        + [whole(bias.shape), per_head(log_dot.shape, 0), per_head(pair_shape, 1)],
-        out_specs=(per_head((heads, toks, width), 0), per_head(pair_shape, 1)),
-        out_shape=(struct((heads, toks, width), F32), struct(pair_shape, F32)),
-        scratch_shapes=[
-            pltpu.VMEM((span, width), BF),
-            pltpu.VMEM((span, width), BF),
-            pltpu.VMEM((toks, toks), BF),
-            pltpu.VMEM((span, toks), BF),
-        ],
-        compiler_params=params(),
-        cost_estimate=cost(8e9, 9e6, 3e6),
-        name="backward",
-    )(qd, kv_low, kv, kv_high, rows, bias, after(log_dot, (qd_low, qd_high)), dkv)
-
-    dkv = pl.pallas_call(
-        functools.partial(rim_kernel, scale, scale2),
-        grid=(heads,),
-        in_specs=[
-            per_head(pair_shape, 1),
-            whole(bias.shape),
-            per_head(pair_shape, 1),
-            per_head(pair_shape, 1),
-            per_head(log_dot.shape, 0),
-            per_head(log_dot.shape, 0),
-            per_head(pair_shape, 1),
-        ],
-        out_specs=per_head(pair_shape, 1),
-        out_shape=struct(pair_shape, F32),
-        scratch_shapes=[
-            pltpu.VMEM((2 * toks, width), BF),
-            pltpu.VMEM((2 * toks, width), BF),
-            pltpu.VMEM((toks, toks + TILE), BF),
-            pltpu.VMEM((toks, toks + TILE), BF),
-        ],
-        compiler_params=params(),
-        cost_estimate=cost(4e9, 8e6, 2e6),
-        name="rim",
-    )(kv, bias, qd_low, qd_high, log_low, log_high, dkv)
+    halves = 2 if heads % 2 == 0 else 1
+    group = heads // halves
+    queries_part, pairs_part = [], []
+    log_late = after(log_dot, (qd_low, qd_high))
+    for half in range(halves):
+        first = half * group
+        dq, pair = pl.pallas_call(
+            functools.partial(backward_kernel, scale, scale2),
+            grid=(group,),
+            in_specs=[per_head(pair_shape, 1, first)] * 4
+            + [per_head(row_shape, 1, first), whole(bias.shape)]
+            + [per_head(log_dot.shape, 0, first), per_head(pair_shape, 1, first)],
+            out_specs=(
+                per_head((group, toks, width), 0),
+                per_head((2, group, toks, width), 1),
+            ),
+            out_shape=(
+                struct((group, toks, width), F32),
+                struct((2, group, toks, width), F32),
+            ),
+            scratch_shapes=[
+                pltpu.VMEM((span, width), BF),
+                pltpu.VMEM((span, width), BF),
+                pltpu.VMEM((toks, toks), BF),
+                pltpu.VMEM((span, toks), BF),
+            ],
+            compiler_params=params(),
+            cost_estimate=cost(4e9, 5e6, 2e6),
+            name="backward",
+        )(qd, kv_low, kv, kv_high, rows, bias, log_late, dkv)
+        queries_part.append(dq)
+        pairs_part.append(pair)
+
+    rim_part = []
+    for half in range(halves):
+        first = half * group
+        rim_part.append(
+            pl.pallas_call(
+                functools.partial(rim_kernel, scale, scale2),
+                grid=(group,),
+                in_specs=[per_head(pair_shape, 1, first), whole(bias.shape)]
+                + [per_head(pair_shape, 1, first)] * 2
+                + [per_head(log_dot.shape, 0, first)] * 2
+                + [per_head((2, group, toks, width), 1)],
+                out_specs=per_head((2, group, toks, width), 1),
+                out_shape=struct((2, group, toks, width), F32),
+                scratch_shapes=[
+                    pltpu.VMEM((2 * toks, width), BF),
+                    pltpu.VMEM((2 * toks, width), BF),
+                    pltpu.VMEM((toks, toks + TILE), BF),
+                    pltpu.VMEM((toks, toks + TILE), BF),
+                ],
+                compiler_params=params(),
+                cost_estimate=cost(2e9, 4e6, 1e6),
+                name="rim",
+            )(kv, bias, qd_low, qd_high, log_low, log_high, pairs_part[half])
+        )
 
     flat_shape = (toks * heads, width)
     steps = 2
     outs = pl.pallas_call(
-        final_kernel,
+        functools.partial(final_kernel, halves),
         grid=(steps,),
         in_specs=[
             pl.BlockSpec((toks // steps, slots), lambda i: (i, 0)),
             pl.BlockSpec((heads, toks // steps, width), lambda i: (0, i, 0)),
-            pl.BlockSpec((heads, toks // steps, width), lambda i: (0, i, 0)),
-            pl.BlockSpec((2, heads, toks // steps, width), lambda i: (0, 0, i, 0)),
             whole(slot_shape),
-        ],
+        ]
+        + [pl.BlockSpec((group, toks // steps, width), lambda i: (0, i, 0))] * halves
+        + [pl.BlockSpec((2, group, toks // steps, width), lambda i: (0, 0, i, 0))] * halves,
         out_specs=[pl.BlockSpec((toks * heads // steps, width), lambda i: (i, 0))] * 4,
         out_shape=[struct(flat_shape, kind) for kind in (BF, F32, F32, F32)],
         scratch_shapes=[pltpu.VMEM((toks * heads // steps, width), F32)],
         compiler_params=params(),
         name="final",
-    )(place, out, dq, dkv, sums[0])
+    )(place, out, sums[0], *queries_part, *rim_part)
     return tuple(x.reshape(toks, heads, width) for x in outs)
 
 

time: 119 us -> 122 us (1.025)
  starting transfers between devices: 37.1 us -> 28.1 us
  waiting for transfers between devices: 18.4 us -> 25.9 us
  Pallas kernels: 51 us -> 55.3 us
  other arithmetic: 7.52 us -> 9.03 us
  local copies, waits for them, and re-layouts: 3.84 us -> 2.42 us
    ppermute x9, starting transfers between devices: 26.2 us -> 16 us  [swap(): return lax.ppermute(value, 'ctx', pairs)]
    ppermute x9, waiting for transfers between devices: 18.3 us -> 25.9 us  [swap(): return lax.ppermute(value, 'ctx', pairs)]
    pallas_call x3 -> x5, Pallas kernels: 20.6 us -> 24.9 us  [the longest x2 12.1 us: shards(): pl.pallas_call(functools.partial(backward_kernel, scale, scale2), grid=(g...]
    add x0 -> x1, other arithmetic: none -> 1.62 us  [shards(): sums = sums + swap(sent, bits - 1)]
    slice x3 -> x2, local copies, waits for them, and re-layouts: 2.23 us -> 0.76 us  [shards(): sums = sums[:half] + swap(sums[half:], stage)]
  transfers between devices with their start and end apart: 15 -> 15, of which waited for: 4 -> 4; matrix products, arithmetic and copies ran while one was open for 7% -> 5% of each run, Pallas kernels for 30% -> 37%
where the time goes in v1:
time: 122 us
  Pallas kernels  55.3 us (45%)
  starting transfers between devices  28.1 us (23%)
  waiting for transfers between devices  25.9 us (21%)
  other arithmetic  9.03 us (7%)
  local copies, waits for them, and re-layouts  2.42 us (2%)
    ppermute x9, waiting for transfers between devices, swap(): return lax.ppermute(value, 'ctx', pairs)  25.9 us
    ppermute x9, starting transfers between devices, swap(): return lax.ppermute(value, 'ctx', pairs)  16 us
    pallas_call x2, Pallas kernels, shards(): pl.pallas_call(functools.partial(backward_kernel, scale, scale2), grid=(g...  12.1 us
    pallas_call x1, Pallas kernels, shards(): pl.pallas_call(functools.partial(forward_kernel, scale2), grid=(heads,),...  9.35 us
    pallas_call x2, Pallas kernels, shards(): pl.pallas_call(functools.partial(rim_kernel, scale, scale2), grid=(group,...  8.96 us
    ppermute x3, starting transfers between devices, from_low(): return lax.ppermute(value, 'ctx', [(i, i + 1) for i in range(devices - 1)])  8.08 us
    pallas_call x1, Pallas kernels, shards(): pl.pallas_call(functools.partial(global_kernel, scale, scale2, slots), gr...  7.07 us
    pallas_call x1, Pallas kernels, shards(): pl.pallas_call(functools.partial(stats_kernel, scale2), grid=(heads,), in...  5.45 us
  transfers between devices with their start and end apart: 15, of which 4 were waited for; matrix products, arithmetic and copies ran while one was open for 5% of the time, Pallas kernels for 37%

profile of v1, /device:TPU:0, one launch (start us, length us, event | category | flops | bytes accessed | tf_op | source)
XLA Modules:
  0.0 121.7 jit_solution(14293499594133987361)
XLA Ops:
  0.6 2.4 %pack_keys.1.kv.refs_4_.own = bf16[2,4,512,128]{3,2,1,0:T(8,128)(2,1)} custom-call(bf16[2048,128]{1,0:T(8,128)(2,1)} %bitcast.16, bf16[2048,128]{1,0:T(8,128)(2,1)} %bitcast.17), custom_call_target="tpu_custom_call" | custom-call | tf_op jit(solution)/shard_map/pack_keys/pallas_call | solution.py:377
  3.1 3.4 %pack_queries.1 = (bf16[2,4,512,128]{3,2,1,0:T(8,128)(2,1)}, bf16[4,4,64,128]{3,2,1,0:T(8,128)(2,1)}) custom-call(bf16[2048,128]{1,0:T(8,128)(2,1)} %bitcast.18, bf16[2048,128]{1,0:T(8,128)(2,1)} %bitcast.19, bf16[2,4,512,128]{3,2,1,0:T(8,128)(2,1)} %pack_keys.1.kv.refs_4_.own, s32[1,256]{1,0:T(1,128)} %bitcast.20), custom_call_target="tpu_custom_call" | custom-call | tf_op jit(solution)/shard_map/pack_queries/pallas_call | solution.py:388
  6.5 2.9 %collective-permute-start = (bf16[1,4,4,64,128]{4,3,2,1,0:T(8,128)(2,1)}, bf16[1,4,4,64,128]{4,3,2,1,0:T(8,128)(2,1)S(1)}, u32[]{:S(2)}, u32[]{:S(2)}) collective-permute-start(bf16[1,4,4,64,128]{4,3,2,1,0:T(8,128)(2,1)} %bitcast.12), channel_id=1, source_target_pairs={{0,8},{4,20},{8,0},{12,28},{16,24},{20,4},{24,16},{28,12},{1,9},{5... | collective-permute-start | bytes 786440 | tf_op jit(solution)/shard_map/ppermute | solution.py:360
  9.4 4.6 %collective-permute-done.refs_1_ = bf16[1,4,4,64,128]{4,3,2,1,0:T(8,128)(2,1)S(1)} collective-permute-done((bf16[1,4,4,64,128]{4,3,2,1,0:T(8,128)(2,1)}, bf16[1,4,4,64,128]{4,3,2,1,0:T(8,128)(2,1)S(1)}, u32[]{:S(2)}, u32[]{:S(2)}) %collective-permute-start) | collective-permute-done | bytes 262176 | tf_op jit(solution)/shard_map/ppermute | solution.py:360
  14.0 1.1 pad_maximum_fusion.1
  15.1 2.1 %collective-permute-start.3 = (bf16[2,4,4,64,128]{4,3,2,1,0:T(8,128)(2,1)S(1)}, bf16[2,4,4,64,128]{4,3,2,1,0:T(8,128)(2,1)S(1)}, u32[]{:S(2)}, u32[]{:S(2)}) collective-permute-start(bf16[2,4,4,64,128]{4,3,2,1,0:T(8,128)(2,1)S(1)} %pad_maximum_fusion.1), channel_id=1, source_target_pairs={{0,16},{4,12},{8,24},{12,4},{16,0},{20,28},{24,8},{28,20},{1,17},{... | collective-permute-start | bytes 1572872 | tf_op jit(solution)/shard_map/ppermute | solution.py:360
  17.2 7.2 %collective-permute-done.3.refs_2_ = bf16[2,4,4,64,128]{4,3,2,1,0:T(8,128)(2,1)S(1)} collective-permute-done((bf16[2,4,4,64,128]{4,3,2,1,0:T(8,128)(2,1)S(1)}, bf16[2,4,4,64,128]{4,3,2,1,0:T(8,128)(2,1)S(1)}, u32[]{:S(2)}, u32[]{:S(2)}) %collective-permute-start.3) | collective-permute-done | bytes 524320 | tf_op jit(solution)/shard_map/ppermute | solution.py:360
  24.4 2.2 %pad_maximum_fusion = bf16[4,4,4,64,128]{4,3,2,1,0:T(8,128)(2,1)} fusion(bf16[2,4,4,64,128]{4,3,2,1,0:T(8,128)(2,1)S(1)} %collective-permute-done.3.refs_2_, bf16[1,4,4,64,128]{4,3,2,1,0:T(8,128)(2,1)S(1)} %collective-permute-done.refs_1_, bf16[1,4,4,64,128]{4,3,2,1,0:T(8,128)(2,1)} %bitcast.14), kind=kLoop, calls=%fused_computation | loop fusion | flops 1048576 | bytes 2097152 | tf_op jit(solution)/shard_map/concatenate | solution.py:401
  26.6 0.0 collective-permute-start.4
  26.6 3.4 %collective-permute-start.1 = (bf16[2,4,512,128]{3,2,1,0:T(8,128)(2,1)}, bf16[2,4,512,128]{3,2,1,0:T(8,128)(2,1)}, u32[]{:S(2)}, u32[]{:S(2)}) collective-permute-start(bf16[2,4,512,128]{3,2,1,0:T(8,128)(2,1)} %pack_keys.1.kv.refs_4_.own), channel_id=1, source_target_pairs={{0,4},{4,8},{8,12},{12,16},{16,20},{20,24},{24,28},{1,5},{5,9},{9,... | collective-permute-start | bytes 3145736 | tf_op jit(solution)/shard_map/ppermute | solution.py:363
  30.0 1.3 %collective-permute-start.2 = (bf16[2,4,512,128]{3,2,1,0:T(8,128)(2,1)}, bf16[2,4,512,128]{3,2,1,0:T(8,128)(2,1)}, u32[]{:S(2)}, u32[]{:S(2)}) collective-permute-start(bf16[2,4,512,128]{3,2,1,0:T(8,128)(2,1)} %pack_keys.1.kv.refs_4_.own), channel_id=1, source_target_pairs={{4,0},{8,4},{12,8},{16,12},{20,16},{24,20},{28,24},{5,1},{9,5},{13... | collective-permute-start | bytes 3145736 | tf_op jit(solution)/shard_map/ppermute | solution.py:366
  31.2 2.6 %masks.1 = (f32[1536,128]{1,0:T(8,128)}, f32[8,1536]{1,0:T(8,128)}, bf16[256,512]{1,0:T(8,128)(2,1)}, bf16[512,256]{1,0:T(8,128)(2,1)}, bf16[512,64]{1,0:T(8,128)(2,1)}) custom-call(s32[1,256]{1,0:T(1,128)} %bitcast.21), custom_call_target="tpu_custom_call" | custom-call | tf_op jit(solution)/shard_map/masks/pallas_call | solution.py:409
  33.9 0.0 collective-permute-done.4.refs_3_
  33.9 5.5 %global_stats.1 = (bf16[4,4,256,128]{3,2,1,0:T(8,128)(2,1)}, f32[1,4,3,256]{3,2,1,0:T(4,128)}) custom-call(bf16[256,512]{1,0:T(8,128)(2,1)} %get-tuple-element.33.compact, bf16[1,4,4,64,128]{4,3,2,1,0:T(8,128)(2,1)} %bitcast.15, bf16[1,4,4,64,128]{4,3,2,1,0:T(8,128)(2,1)} %copy-done.1, bf16[2,4,4,64,128]{4,3,2,1,0:T(8,128)(2,1)} %copy-done.2, ...), custom_call_target="tpu_custom_call" | custom-call | flops 2700000000 | bytes 4000000 | tf_op jit(solution)/shard_map/global_stats/pallas_call | solution.py:423
  39.4 2.9 %collective-permute-start.5 = (f32[1,4,3,256]{3,2,1,0:T(4,128)}, f32[1,4,3,256]{3,2,1,0:T(4,128)S(1)}, u32[]{:S(2)}, u32[]{:S(2)}) collective-permute-start(f32[1,4,3,256]{3,2,1,0:T(4,128)} %get-tuple-element.38), channel_id=1, source_target_pairs={{0,8},{4,20},{8,0},{12,28},{16,24},{20,4},{24,16},{28,12},{1,9},{5... | collective-permute-start | bytes 36872 | tf_op jit(solution)/shard_map/ppermute | solution.py:360
  42.2 13.9 %collective-permute-done.5 = f32[1,4,3,256]{3,2,1,0:T(4,128)S(1)} collective-permute-done((f32[1,4,3,256]{3,2,1,0:T(4,128)}, f32[1,4,3,256]{3,2,1,0:T(4,128)S(1)}, u32[]{:S(2)}, u32[]{:S(2)}) %collective-permute-start.5) | collective-permute-done | bytes 12320 | tf_op jit(solution)/shard_map/ppermute | solution.py:360
  56.1 0.7 pad_maximum_fusion.4
  56.8 0.1 collective-permute-start.6
  56.9 0.0 collective-permute-done.1.left
  56.9 2.3 %collective-permute-start.11 = (bf16[2,4,512,128]{3,2,1,0:T(8,128)(2,1)}, bf16[2,4,512,128]{3,2,1,0:T(8,128)(2,1)}, u32[]{:S(2)}, u32[]{:S(2)}) collective-permute-start(bf16[2,4,512,128]{3,2,1,0:T(8,128)(2,1)} %get-tuple-element.43.qd), channel_id=1, source_target_pairs={{0,4},{4,8},{8,12},{12,16},{16,20},{20,24},{24,28},{1,5},{5,9},{9,... | collective-permute-start | bytes 3145736 | tf_op jit(solution)/shard_map/ppermute | solution.py:363
  59.2 1.3 %collective-permute-start.12 = (bf16[2,4,512,128]{3,2,1,0:T(8,128)(2,1)}, bf16[2,4,512,128]{3,2,1,0:T(8,128)(2,1)}, u32[]{:S(2)}, u32[]{:S(2)}) collective-permute-start(bf16[2,4,512,128]{3,2,1,0:T(8,128)(2,1)} %get-tuple-element.43.qd), channel_id=1, source_target_pairs={{4,0},{8,4},{12,8},{16,12},{20,16},{24,20},{28,24},{5,1},{9,5},{13... | collective-permute-start | bytes 3145736 | tf_op jit(solution)/shard_map/ppermute | solution.py:366
  60.5 0.3 collective-permute-done.6
  60.8 0.7 pad_maximum_fusion.3
  61.5 2.2 %collective-permute-start.7 = (f32[4,4,3,256]{3,2,1,0:T(4,128)S(1)}, f32[4,4,3,256]{3,2,1,0:T(4,128)S(1)}, u32[]{:S(2)}, u32[]{:S(2)}) collective-permute-start(f32[4,4,3,256]{3,2,1,0:T(4,128)S(1)} %pad_maximum_fusion.3), channel_id=1, source_target_pairs={{0,4},{4,0},{8,12},{12,8},{16,20},{20,16},{24,28},{28,24},{1,5},{5... | collective-permute-start | bytes 147464 | tf_op jit(solution)/shard_map/ppermute | solution.py:360
  63.7 9.3 %forward.1 = (bf16[4,512,128]{2,1,0:T(8,128)(2,1)}, f32[4,2,512]{2,1,0:T(2,128)}) custom-call(bf16[2,4,512,128]{3,2,1,0:T(8,128)(2,1)} %get-tuple-element.43.qd, bf16[2,4,512,128]{3,2,1,0:T(8,128)(2,1)} %collective-permute-done.1.left, bf16[2,4,512,128]{3,2,1,0:T(8,128)(2,1)} %pack_keys.1.kv.refs_4_.own, ...), custom_call_target="tpu_custom_call" | custom-call | flops 4000000000 | bytes 5000000 | tf_op jit(solution)/shard_map/forward/pallas_call | solution.py:446
  73.1 0.7 pad_maximum_fusion.2.stats
  73.8 7.1 %globals.1 = (f32[2,4,512,128]{3,2,1,0:T(8,128)}, bf16[4,4,4,64,128]{4,3,2,1,0:T(8,128)(2,1)}, bf16[4,4,4,64,128]{4,3,2,1,0:T(8,128)(2,1)}) custom-call(bf16[2,4,512,128]{3,2,1,0:T(8,128)(2,1)} %get-tuple-element.43.qd, bf16[2,4,512,128]{3,2,1,0:T(8,128)(2,1)} %pack_keys.1.kv.refs_4_.own, bf16[4,4,256,128]{3,2,1,0:T(8,128)(2,1)} %get-tuple-element.34.rows, ...), custom_call_target="tpu_custom_call" | custom-call | flops 4000000000 | bytes 9000000 | tf_op jit(solution)/shard_map/globals/pallas_call | solution.py:465
  80.8 0.0 collective-permute-start.8
  80.9 2.4 %collective-permute-start.13 = (f32[4,2,512]{2,1,0:T(2,128)S(1)}, f32[4,2,512]{2,1,0:T(2,128)S(1)}, u32[]{:S(2)}, u32[]{:S(2)}) collective-permute-start(f32[4,2,512]{2,1,0:T(2,128)S(1)} %copy-done.4), channel_id=1, source_target_pairs={{0,4},{4,8},{8,12},{12,16},{16,20},{20,24},{24,28},{1,5},{5,9},{9,... | collective-permute-start | bytes 49160 | tf_op jit(solution)/shard_map/ppermute | solution.py:363
  83.3 1.5 %collective-permute-start.14 = (f32[4,2,512]{2,1,0:T(2,128)S(1)}, f32[4,2,512]{2,1,0:T(2,128)S(1)}, u32[]{:S(2)}, u32[]{:S(2)}) collective-permute-start(f32[4,2,512]{2,1,0:T(2,128)S(1)} %copy-done.4), channel_id=1, source_target_pairs={{4,0},{8,4},{12,8},{16,12},{20,16},{24,20},{28,24},{5,1},{9,5},{13... | collective-permute-start | bytes 49160 | tf_op jit(solution)/shard_map/ppermute | solution.py:366
  84.7 0.0 collective-permute-done.11.qd_low
  84.8 0.0 collective-permute-done.12.qd_high
  84.8 1.6 %add.9 = bf16[4,4,4,64,128]{4,3,2,1,0:T(8,128)(2,1)S(1)} add(bf16[4,4,4,64,128]{4,3,2,1,0:T(8,128)(2,1)} %get-tuple-element.40, bf16[4,4,4,64,128]{4,3,2,1,0:T(8,128)(2,1)S(1)} %collective-permute-done.8) | non-fusion elementwise | flops 524288 | bytes 3145728 | tf_op jit(solution)/shard_map/add | solution.py:483
  86.4 1.0 copy-done
  87.5 5.8 %collective-permute-start.9 = (bf16[2,4,4,64,128]{4,3,2,1,0:T(8,128)(2,1)S(1)}, bf16[2,4,4,64,128]{4,3,2,1,0:T(8,128)(2,1)}, u32[]{:S(2)}, u32[]{:S(2)}) collective-permute-start(bf16[2,4,4,64,128]{4,3,2,1,0:T(8,128)(2,1)S(1)} %slice.17), channel_id=1, source_target_pairs={{0,16},{4,12},{8,24},{12,4},{16,0},{20,28},{24,8},{28,20},{1,17},{... | collective-permute-start | bytes 1572872 | tf_op jit(solution)/shard_map/ppermute | solution.py:360
  93.3 6.1 %backward.2 = (f32[2,512,128]{2,1,0:T(8,128)}, f32[2,2,512,128]{3,2,1,0:T(8,128)}) custom-call(bf16[2,4,512,128]{3,2,1,0:T(8,128)(2,1)} %get-tuple-element.43.qd, bf16[2,4,512,128]{3,2,1,0:T(8,128)(2,1)} %collective-permute-done.1.left, bf16[2,4,512,128]{3,2,1,0:T(8,128)(2,1)} %pack_keys.1.kv.refs_4_.own, ...), custom_call_target="tpu_custom_call" | custom-call | flops 4000000000 | bytes 5000000 | tf_op jit(solution)/shard_map/backward/pallas_call | solution.py:494
  99.4 6.0 %backward.3 = (f32[2,512,128]{2,1,0:T(8,128)}, f32[2,2,512,128]{3,2,1,0:T(8,128)}) custom-call(bf16[2,4,512,128]{3,2,1,0:T(8,128)(2,1)} %get-tuple-element.43.qd, bf16[2,4,512,128]{3,2,1,0:T(8,128)(2,1)} %collective-permute-done.1.left, bf16[2,4,512,128]{3,2,1,0:T(8,128)(2,1)} %pack_keys.1.kv.refs_4_.own, ...), custom_call_target="tpu_custom_call" | custom-call | flops 4000000000 | bytes 5000000 | tf_op jit(solution)/shard_map/backward/pallas_call | solution.py:494
  105.4 0.0 collective-permute-done.9
  105.4 1.3 %slice_add_fusion = bf16[2,4,4,64,128]{4,3,2,1,0:T(8,128)(2,1)S(1)} fusion(bf16[2,4,4,64,128]{4,3,2,1,0:T(8,128)(2,1)} %collective-permute-done.9, bf16[4,4,4,64,128]{4,3,2,1,0:T(8,128)(2,1)} %copy-done), kind=kLoop, calls=%fused_computation.1 | loop fusion | flops 262144 | bytes 1572864 | tf_op jit(solution)/shard_map/add | solution.py:486
  106.7 0.7 slice.19
  107.4 0.0 collective-permute-done.14.log_high
  107.4 0.0 copy-start.6
  107.5 0.6 copy-done.5
  108.0 0.0 copy-done.6
  108.0 4.5 %rim.2.refs_2_ = f32[2,2,512,128]{3,2,1,0:T(8,128)} custom-call(bf16[2,4,512,128]{3,2,1,0:T(8,128)(2,1)} %pack_keys.1.kv.refs_4_.own, f32[1536,128]{1,0:T(8,128)} %get-tuple-element.42.bias, bf16[2,4,512,128]{3,2,1,0:T(8,128)(2,1)} %collective-permute-done.11.qd_low, bf16[2,4,512,128]{3,2,1,0:T(8,128)(2,1)} %collective-permute-done.12.qd_high, ...), custom_call_target="tpu_custom_call" | custom-call | flops 2000000000 | bytes 4000000 | tf_op jit(solution)/shard_map/rim/pallas_call | solution.py:525
  112.5 4.5 %rim.3.refs_3_ = f32[2,2,512,128]{3,2,1,0:T(8,128)} custom-call(bf16[2,4,512,128]{3,2,1,0:T(8,128)(2,1)} %pack_keys.1.kv.refs_4_.own, f32[1536,128]{1,0:T(8,128)} %get-tuple-element.42.bias, bf16[2,4,512,128]{3,2,1,0:T(8,128)(2,1)} %collective-permute-done.11.qd_low, bf16[2,4,512,128]{3,2,1,0:T(8,128)(2,1)} %collective-permute-done.12.qd_high, ...), custom_call_target="tpu_custom_call" | custom-call | flops 2000000000 | bytes 4000000 | tf_op jit(solution)/shard_map/rim/pallas_call | solution.py:525
  117.0 0.7 fusion.sums
  117.7 3.9 %final.1 = (bf16[2048,128]{1,0:T(8,128)(2,1)}, f32[2048,128]{1,0:T(8,128)}, f32[2048,128]{1,0:T(8,128)}, f32[2048,128]{1,0:T(8,128)}) custom-call(bf16[512,64]{1,0:T(8,128)(2,1)} %get-tuple-element.29.place, bf16[4,512,128]{2,1,0:T(8,128)(2,1)} %get-tuple-element.36.out, bf16[4,4,64,128]{3,2,1,0:T(8,128)(2,1)} %fusion.sums, ...), custom_call_target="tpu_custom_call" | custom-call | tf_op jit(solution)/shard_map/final/pallas_call | solution.py:548
  (17 shorter events, 0.1 us)
Async XLA Ops:
  6.5 7.5 %collective-permute-start = (bf16[1,4,4,64,128]{4,3,2,1,0:T(8,128)(2,1)}, bf16[1,4,4,64,128]{4,3,2,1,0:T(8,128)(2,1)S(1)}, u32[]{:S(2)}, u32[]{:S(2)}) collective-permute-start(bf16[1,4,4,64,128]{4,3,2,1,0:T(8,128)(2,1)} %bitcast.12), channel_id=1, source_target_pairs={{0,8},{4,20},{8,0},{12,28},{16,24},{20,4},{24,16},{28,12},{1,9},{5... | collective-permute-start | bytes 786440 | tf_op jit(solution)/shard_map/ppermute | solution.py:360
  14.0 19.9 %copy-start.1 = (bf16[1,4,4,64,128]{4,3,2,1,0:T(8,128)(2,1)}, bf16[1,4,4,64,128]{4,3,2,1,0:T(8,128)(2,1)S(1)}, u32[]{:S(2)}) copy-start(bf16[1,4,4,64,128]{4,3,2,1,0:T(8,128)(2,1)S(1)} %collective-permute-done.refs_1_) | copy-start | bytes 786436
  15.1 9.3 %collective-permute-start.3 = (bf16[2,4,4,64,128]{4,3,2,1,0:T(8,128)(2,1)S(1)}, bf16[2,4,4,64,128]{4,3,2,1,0:T(8,128)(2,1)S(1)}, u32[]{:S(2)}, u32[]{:S(2)}) collective-permute-start(bf16[2,4,4,64,128]{4,3,2,1,0:T(8,128)(2,1)S(1)} %pad_maximum_fusion.1), channel_id=1, source_target_pairs={{0,16},{4,12},{8,24},{12,4},{16,0},{20,28},{24,8},{28,20},{1,17},{... | collective-permute-start | bytes 1572872 | tf_op jit(solution)/shard_map/ppermute | solution.py:360
  24.4 9.5 %copy-start.2 = (bf16[2,4,4,64,128]{4,3,2,1,0:T(8,128)(2,1)}, bf16[2,4,4,64,128]{4,3,2,1,0:T(8,128)(2,1)S(1)}, u32[]{:S(2)}) copy-start(bf16[2,4,4,64,128]{4,3,2,1,0:T(8,128)(2,1)S(1)} %collective-permute-done.3.refs_2_) | copy-start | bytes 1572868
  26.6 7.3 %collective-permute-start.4 = (bf16[4,4,4,64,128]{4,3,2,1,0:T(8,128)(2,1)}, bf16[4,4,4,64,128]{4,3,2,1,0:T(8,128)(2,1)}, u32[]{:S(2)}, u32[]{:S(2)}) collective-permute-start(bf16[4,4,4,64,128]{4,3,2,1,0:T(8,128)(2,1)} %pad_maximum_fusion), channel_id=1, source_target_pairs={{0,4},{4,0},{8,12},{12,8},{16,20},{20,16},{24,28},{28,24},{1,5},{5... | collective-permute-start | bytes 3145736 | tf_op jit(solution)/shard_map/ppermute | solution.py:360
  26.6 30.3 %collective-permute-start.1 = (bf16[2,4,512,128]{3,2,1,0:T(8,128)(2,1)}, bf16[2,4,512,128]{3,2,1,0:T(8,128)(2,1)}, u32[]{:S(2)}, u32[]{:S(2)}) collective-permute-start(bf16[2,4,512,128]{3,2,1,0:T(8,128)(2,1)} %pack_keys.1.kv.refs_4_.own), channel_id=1, source_target_pairs={{0,4},{4,8},{8,12},{12,16},{16,20},{20,24},{24,28},{1,5},{5,9},{9,... | collective-permute-start | bytes 3145736 | tf_op jit(solution)/shard_map/ppermute | solution.py:363
  30.0 27.0 %collective-permute-start.2 = (bf16[2,4,512,128]{3,2,1,0:T(8,128)(2,1)}, bf16[2,4,512,128]{3,2,1,0:T(8,128)(2,1)}, u32[]{:S(2)}, u32[]{:S(2)}) collective-permute-start(bf16[2,4,512,128]{3,2,1,0:T(8,128)(2,1)} %pack_keys.1.kv.refs_4_.own), channel_id=1, source_target_pairs={{4,0},{8,4},{12,8},{16,12},{20,16},{24,20},{28,24},{5,1},{9,5},{13... | collective-permute-start | bytes 3145736 | tf_op jit(solution)/shard_map/ppermute | solution.py:366
  39.4 16.7 %collective-permute-start.5 = (f32[1,4,3,256]{3,2,1,0:T(4,128)}, f32[1,4,3,256]{3,2,1,0:T(4,128)S(1)}, u32[]{:S(2)}, u32[]{:S(2)}) collective-permute-start(f32[1,4,3,256]{3,2,1,0:T(4,128)} %get-tuple-element.38), channel_id=1, source_target_pairs={{0,8},{4,20},{8,0},{12,28},{16,24},{20,4},{24,16},{28,12},{1,9},{5... | collective-permute-start | bytes 36872 | tf_op jit(solution)/shard_map/ppermute | solution.py:360
  56.8 4.0 %collective-permute-start.6 = (f32[2,4,3,256]{3,2,1,0:T(4,128)S(1)}, f32[2,4,3,256]{3,2,1,0:T(4,128)S(1)}, u32[]{:S(2)}, u32[]{:S(2)}) collective-permute-start(f32[2,4,3,256]{3,2,1,0:T(4,128)S(1)} %pad_maximum_fusion.4), channel_id=1, source_target_pairs={{0,16},{4,12},{8,24},{12,4},{16,0},{20,28},{24,8},{28,20},{1,17},{... | collective-permute-start | bytes 73736 | tf_op jit(solution)/shard_map/ppermute | solution.py:360
  56.9 27.8 %collective-permute-start.11 = (bf16[2,4,512,128]{3,2,1,0:T(8,128)(2,1)}, bf16[2,4,512,128]{3,2,1,0:T(8,128)(2,1)}, u32[]{:S(2)}, u32[]{:S(2)}) collective-permute-start(bf16[2,4,512,128]{3,2,1,0:T(8,128)(2,1)} %get-tuple-element.43.qd), channel_id=1, source_target_pairs={{0,4},{4,8},{8,12},{12,16},{16,20},{20,24},{24,28},{1,5},{5,9},{9,... | collective-permute-start | bytes 3145736 | tf_op jit(solution)/shard_map/ppermute | solution.py:363
  59.2 25.5 %collective-permute-start.12 = (bf16[2,4,512,128]{3,2,1,0:T(8,128)(2,1)}, bf16[2,4,512,128]{3,2,1,0:T(8,128)(2,1)}, u32[]{:S(2)}, u32[]{:S(2)}) collective-permute-start(bf16[2,4,512,128]{3,2,1,0:T(8,128)(2,1)} %get-tuple-element.43.qd), channel_id=1, source_target_pairs={{4,0},{8,4},{12,8},{16,12},{20,16},{24,20},{28,24},{5,1},{9,5},{13... | collective-permute-start | bytes 3145736 | tf_op jit(solution)/shard_map/ppermute | solution.py:366
  61.5 11.5 %collective-permute-start.7 = (f32[4,4,3,256]{3,2,1,0:T(4,128)S(1)}, f32[4,4,3,256]{3,2,1,0:T(4,128)S(1)}, u32[]{:S(2)}, u32[]{:S(2)}) collective-permute-start(f32[4,4,3,256]{3,2,1,0:T(4,128)S(1)} %pad_maximum_fusion.3), channel_id=1, source_target_pairs={{0,4},{4,0},{8,12},{12,8},{16,20},{20,16},{24,28},{28,24},{1,5},{5... | collective-permute-start | bytes 147464 | tf_op jit(solution)/shard_map/ppermute | solution.py:360
  63.7 9.4 %copy-start.3 = (f32[1,4,3,256]{3,2,1,0:T(4,128)S(1)}, f32[1,4,3,256]{3,2,1,0:T(4,128)}, u32[]{:S(2)}) copy-start(f32[1,4,3,256]{3,2,1,0:T(4,128)} %get-tuple-element.38) | copy-start | bytes 36868
  73.8 7.1 %copy-start.4 = (f32[4,2,512]{2,1,0:T(2,128)S(1)}, f32[4,2,512]{2,1,0:T(2,128)}, u32[]{:S(2)}) copy-start(f32[4,2,512]{2,1,0:T(2,128)} %get-tuple-element.44.log_dot) | copy-start | bytes 49156
  80.8 3.9 %collective-permute-start.8 = (bf16[4,4,4,64,128]{4,3,2,1,0:T(8,128)(2,1)}, bf16[4,4,4,64,128]{4,3,2,1,0:T(8,128)(2,1)S(1)}, u32[]{:S(2)}, u32[]{:S(2)}) collective-permute-start(bf16[4,4,4,64,128]{4,3,2,1,0:T(8,128)(2,1)} %get-tuple-element.41), channel_id=1, source_target_pairs={{0,4},{4,0},{8,12},{12,8},{16,20},{20,16},{24,28},{28,24},{1,5},{5... | collective-permute-start | bytes 3145736 | tf_op jit(solution)/shard_map/ppermute | solution.py:360
  80.9 26.5 %collective-permute-start.13 = (f32[4,2,512]{2,1,0:T(2,128)S(1)}, f32[4,2,512]{2,1,0:T(2,128)S(1)}, u32[]{:S(2)}, u32[]{:S(2)}) collective-permute-start(f32[4,2,512]{2,1,0:T(2,128)S(1)} %copy-done.4), channel_id=1, source_target_pairs={{0,4},{4,8},{8,12},{12,16},{16,20},{20,24},{24,28},{1,5},{5,9},{9,... | collective-permute-start | bytes 49160 | tf_op jit(solution)/shard_map/ppermute | solution.py:363
  83.3 24.2 %collective-permute-start.14 = (f32[4,2,512]{2,1,0:T(2,128)S(1)}, f32[4,2,512]{2,1,0:T(2,128)S(1)}, u32[]{:S(2)}, u32[]{:S(2)}) collective-permute-start(f32[4,2,512]{2,1,0:T(2,128)S(1)} %copy-done.4), channel_id=1, source_target_pairs={{4,0},{8,4},{12,8},{16,12},{20,16},{24,20},{28,24},{5,1},{9,5},{13... | collective-permute-start | bytes 49160 | tf_op jit(solution)/shard_map/ppermute | solution.py:366
  86.4 1.1 copy-start
  87.5 17.9 %collective-permute-start.9 = (bf16[2,4,4,64,128]{4,3,2,1,0:T(8,128)(2,1)S(1)}, bf16[2,4,4,64,128]{4,3,2,1,0:T(8,128)(2,1)}, u32[]{:S(2)}, u32[]{:S(2)}) collective-permute-start(bf16[2,4,4,64,128]{4,3,2,1,0:T(8,128)(2,1)S(1)} %slice.17), channel_id=1, source_target_pairs={{0,16},{4,12},{8,24},{12,4},{16,0},{20,28},{24,8},{28,20},{1,17},{... | collective-permute-start | bytes 1572872 | tf_op jit(solution)/shard_map/ppermute | solution.py:360
  107.4 9.6 %collective-permute-start.10 = (bf16[1,4,4,64,128]{4,3,2,1,0:T(8,128)(2,1)}, bf16[1,4,4,64,128]{4,3,2,1,0:T(8,128)(2,1)S(1)}, u32[]{:S(2)}, u32[]{:S(2)}) collective-permute-start(bf16[1,4,4,64,128]{4,3,2,1,0:T(8,128)(2,1)} %slice.19), channel_id=1, source_target_pairs={{0,8},{4,20},{8,0},{12,28},{16,24},{20,4},{24,16},{28,12},{1,9},{5... | collective-permute-start | bytes 786440 | tf_op jit(solution)/shard_map/ppermute | solution.py:360
  107.4 0.6 copy-start.5
  107.4 0.6 copy-start.6
